TPU v7x, 128 devices: a whole 4x4x4 slice. The times are simulated.
128 devices in a mesh: pair: 32 (over y, x, core), rep: 4 (over z).
Axes of the slice: x: 4, y: 4, z: 4, core: 2. Of those that a mesh axis runs over, the one named last changes fastest.
Arguments:
- amplitude: bfloat16 [1600, 16384], P('pair', 'rep'), may hold values from -6 to 6
- tile_mask: int32 [40, 40, 2, 2], replicated, may hold values 0 or 1
- ladder_ints: bfloat16 [16384, 16384], P('rep', 'pair'), may hold values from -0.046875 to 0.046875
- cycle_ints: bfloat16 [128, 40, 5120], P('pair', None, 'rep'), may hold values from -0.078125 to 0.078125
- coulomb: bfloat16 [40, 40, 16384], P('rep', None, 'pair'), may hold values from -6 to 6
- eps_occ: float32 [40], replicated, may hold values from -2 to -0.5
- eps_vir: float32 [128], replicated, may hold values from 0.5 to 3
Outputs:
- amp_new: bfloat16 [40, 40, 16384], P('rep', None, 'pair')
All inputs are finite; a program needn't handle non-finite values.
Results may differ from a plain program's by a relative error of at most 0.001.
Values may be sent and summed in bfloat16 or wider, within the bound.
A program may use at most 128 MiB of HBM per device.

v0:
```python
import jax
import jax.numpy as jnp
from jax import lax
from jax.sharding import PartitionSpec as P


def shards(amplitude, tile_mask, ladder_ints, cycle_ints, coulomb, eps_occ, eps_vir):
    n_rep = lax.axis_size("rep")
    pair_at = lax.axis_index("pair")
    rep_at = lax.axis_index("rep")
    occ = tile_mask.shape[0]
    tiles = tile_mask.shape[2]
    virt = eps_vir.shape[0]
    tile_len = virt // tiles
    rows_loc = amplitude.shape[0]
    c_loc = amplitude.shape[1] // virt
    a_loc = cycle_ints.shape[0]
    ab_loc = coulomb.shape[2]
    tile_ids = jnp.arange(tiles, dtype=jnp.int32)
    c_tile = (rep_at * c_loc + jnp.arange(c_loc, dtype=jnp.int32)) // tile_len
    d_tile = jnp.arange(virt, dtype=jnp.int32) // tile_len
    c_onehot = (c_tile[:, None] == tile_ids[None, :]).astype(jnp.float32)
    d_onehot = (d_tile[:, None] == tile_ids[None, :]).astype(jnp.float32)
    mask_rows = lax.dynamic_slice_in_dim(
        tile_mask.reshape(occ * occ, tiles, tiles), pair_at * rows_loc, rows_loc, 0
    ).astype(jnp.float32)
    expanded = jnp.einsum("rCD,cC,dD->rcd", mask_rows, c_onehot, d_onehot).reshape(
        rows_loc, c_loc * virt
    )
    screened = amplitude * expanded.astype(jnp.bfloat16)
    gathered = lax.all_gather(screened, "pair", axis=0, tiled=True)
    ladder = jnp.dot(gathered, ladder_ints, preferred_element_type=jnp.float32).reshape(
        occ, occ, ab_loc
    )
    cycle_tr = jnp.einsum(
        "aick,kjcb->jiab",
        cycle_ints.reshape(a_loc, occ, c_loc, occ),
        gathered.reshape(occ, occ, c_loc, virt),
        preferred_element_type=jnp.float32,
    )
    direct = jnp.transpose(cycle_tr, (1, 0, 2, 3)).reshape(occ, occ, ab_loc)
    swapped = lax.all_to_all(cycle_tr, "pair", split_axis=3, concat_axis=2, tiled=True)
    mirror = jnp.transpose(swapped, (0, 1, 3, 2)).reshape(occ, occ, ab_loc)
    totals = lax.psum(((ladder + direct + mirror,)[0],), "rep")
    summed = tuple(
        (
            lax.dynamic_slice_in_dim(
                item, rep_at * (item.shape[0] // n_rep), item.shape[0] // n_rep, 0
            )
            for item in totals
        )
    )[0]
    occ_loc = occ // n_rep
    occ_mine = lax.dynamic_slice_in_dim(eps_occ, rep_at * occ_loc, occ_loc, 0)
    vir_first = lax.dynamic_slice_in_dim(eps_vir, pair_at * a_loc, a_loc, 0)
    vir_pairs = (vir_first[:, None] + eps_vir[None, :]).reshape(ab_loc)
    denom = vir_pairs[None, None, :] - occ_mine[:, None, None] - eps_occ[None, :, None]
    residual = coulomb.astype(jnp.float32) + summed
    return (residual / denom).astype(jnp.bfloat16)


def solution(mesh):
    placed = (
        P("pair", "rep"),
        P(),
        P("rep", "pair"),
        P("pair", None, "rep"),
        P("rep", None, "pair"),
        P(),
        P(),
    )
    return jax.shard_map(
        shards, mesh=mesh, in_specs=placed, out_specs=P("rep", None, "pair"), check_vma=False
    )
```

profile of v0, /device:TPU:1, one launch (start us, length us, event | category | flops | bytes accessed | tf_op | source)
XLA Modules:
  0.0 323.0 jit_solution(1377625520050462848)
XLA Ops:
  6.6 1.0 copy.30
  7.5 0.1 reshape.112
  7.6 0.2 fusion.5
  7.8 0.4 fusion.3
  8.3 0.2 copy.34
  8.5 0.8 multiply_bitcast_fusion
  9.4 2.4 reshape.101
  11.8 3.3 %copy.22 = bf16[4,40,32,40]{1,2,3,0:T(8,128)(2,1)} copy(bf16[4,40,32,40]{3,2,1,0:T(8,128)(2,1)S(1)} %reshape.101) | data formatting | bytes 819200 | tf_op jit(solution)/shard_map/reshape | solution.py:37
  15.1 65.9 %all-gather.3.cloned.1.call-done = bf16[32,50,4096]{2,1,0:T(8,128)(2,1)} async-done(((bf16[1,50,4096]{2,1,0:T(8,128)(2,1)}), bf16[32,50,4096]{2,1,0:T(8,128)(2,1)}) %all-gather.3.cloned.1.call-update) | async-done | bytes 13107216 | tf_op jit(solution)/shard_map/all_gather | solution.py:31
  80.9 18.2 %reshape.100 = bf16[40,40,32,128]{3,2,1,0:T(8,128)(2,1)} reshape(bf16[32,50,4096]{2,1,0:T(8,128)(2,1)} %all-gather.3.cloned.1.call-done) | data formatting | bytes 26214400 | tf_op jit(solution)/shard_map/reshape | solution.py:38
  99.1 6.4 %fusion = f32[40,128,4,40,1]{1,3,4,2,0:T(8,128)S(1)} fusion(bf16[4,40,32,40]{1,2,3,0:T(8,128)(2,1)} %copy.22, bf16[40,40,32,128]{3,2,1,0:T(8,128)(2,1)} %reshape.100), kind=kOutput, calls=%fused_computation | convolution fusion | flops 2097152000 | bytes 16793600 | tf_op jit(solution)/shard_map/aick,kjcb->jiab/dot_general | solution.py:35
  105.6 7.0 %copy.24 = f32[40,40,4,128]{1,2,0,3:T(4,128)} copy(f32[40,40,4,128]{3,1,2,0:T(8,128)S(1)} %bitcast.47) | data formatting | bytes 6553600 | tf_op jit(solution)/shard_map/aick,kjcb->jiab/transpose | solution.py:35
  112.6 17.0 %reshape.113 = f32[32,1,25600]{2,1,0:T(1,128)} reshape(f32[128,40,4,40]{3,2,1,0:T(4,128)} %bitcast.46) | data formatting | bytes 6553600
  129.6 5.5 %all-to-all-start = ((f32[32,1,25600]{2,1,0:T(1,128)}), f32[32,1,25600]{2,1,0:T(1,128)}, u32[]{:S(2)}, u32[]{:S(2)}) async-start(f32[32,1,25600]{2,1,0:T(1,128)} %reshape.113), calls=%async_computation | async-start | bytes 6553600 | tf_op jit(solution)/shard_map/all_to_all | solution.py:42
  135.1 2.5 copy.23
  137.6 3.4 %reshape.102 = f32[40,40,512]{2,1,0:T(8,128)S(1)} reshape(f32[40,40,4,128]{3,2,1,0:T(4,128)} %copy.23) | data formatting | bytes 6553600 | tf_op jit(solution)/shard_map/reshape | solution.py:41
  141.0 13.3 %reshape.105 = bf16[1600,4096]{1,0:T(8,128)(2,1)} reshape(bf16[32,50,4096]{2,1,0:T(8,128)(2,1)} %all-gather.3.cloned.1.call-done) | data formatting | bytes 26214400
  154.3 12.4 %fusion.17 = f32[1600,512]{1,0:T(8,128)} fusion(bf16[1600,4096]{1,0:T(8,128)(2,1)} %reshape.105, bf16[4096,512]{1,0:T(8,128)(2,1)} %param.9), kind=kOutput, calls=%fused_computation.31 | convolution fusion | flops 6710886400 | bytes 20578304 | tf_op jit(solution)/shard_map/dot_general | solution.py:32
  166.7 8.9 %all-to-all-done = f32[32,1,25600]{2,1,0:T(1,128)} async-done(((f32[32,1,25600]{2,1,0:T(1,128)}), f32[32,1,25600]{2,1,0:T(1,128)}, u32[]{:S(2)}, u32[]{:S(2)}) %all-to-all-start) | async-done | bytes 3276832 | tf_op jit(solution)/shard_map/all_to_all | solution.py:42
  175.6 0.5 broadcast.92
  176.1 12.0 %reduce = f32[32,25600]{1,0:T(8,128)} reduce(f32[32,1,25600]{2,1,0:T(1,128)} %all-to-all-done, f32[]{:T(128)} %broadcast.92), dimensions={1}, to_apply=%all_to_all.13.reduce_sub_computation | reduce | bytes 6553604 | tf_op jit(solution)/shard_map/all_to_all | solution.py:42
  188.1 18.5 %reshape.114 = f32[128,40,4,40]{3,2,1,0:T(4,128)} reshape(f32[32,25600]{1,0:T(8,128)} %reduce) | data formatting | bytes 6553600
  206.6 4.7 %copy.25 = f32[40,40,4,128]{1,0,3,2:T(8,128)S(1)} copy(f32[40,40,4,128]{1,2,0,3:T(4,128)} %bitcast.43) | data formatting | bytes 6553600 | tf_op jit(solution)/shard_map/all_to_all | solution.py:42
  211.3 5.0 %copy.26 = f32[40,40,32,4,4]{1,0,4,3,2:T(8,128)} copy(f32[40,40,32,4,4]{1,0,4,2,3:T(8,128)S(1)} %bitcast.44) | data formatting | bytes 6553600 | tf_op jit(solution)/shard_map/all_to_all | solution.py:42
  216.3 9.3 %copy.27 = f32[40,40,4,128]{3,2,1,0:T(4,128)} copy(f32[40,40,4,128]{1,0,2,3:T(8,128)} %bitcast.45) | data formatting | bytes 6553600 | tf_op jit(solution)/shard_map/transpose | solution.py:43
  225.6 5.1 %reshape.103 = f32[40,40,512]{2,1,0:T(8,128)} reshape(f32[40,40,4,128]{3,2,1,0:T(4,128)} %copy.27) | data formatting | bytes 6553600 | tf_op jit(solution)/shard_map/reshape | solution.py:43
  230.7 5.8 %add_add_fusion = f32[40,40,512]{2,1,0:T(8,128)} fusion(f32[40,40,512]{2,1,0:T(8,128)} %reshape.103, f32[40,40,512]{2,1,0:T(8,128)} %bitcast.49, f32[40,40,512]{2,1,0:T(8,128)S(1)} %reshape.102), kind=kLoop, calls=%fused_computation.2 | loop fusion | flops 1638400 | bytes 13107200 | tf_op jit(solution)/shard_map/add | solution.py:44
  236.6 0.6 copy-done.4
  237.2 0.1 dynamic_slice.14
  237.4 0.1 broadcast_subtract_fusion
  237.5 76.6 %all-reduce.2.cloned.1.call-done = f32[40,40,512]{2,1,0:T(8,128)} async-done(((f32[40,40,512]{2,1,0:T(8,128)}), f32[40,40,512]{2,1,0:T(8,128)}) %all-reduce.2.cloned.1.call-update) | async-done | bytes 3276816 | tf_op jit(solution)/shard_map/psum | solution.py:44
  314.1 2.1 divide_convert_fusion
  (19 shorter events, 0.3 us)
Async XLA Ops:
  6.5 2.0 copy-start
  6.5 2.8 copy-start.2
  6.5 74.4 %all-gather.3.cloned.1.call-start = ((), (), s32[]{:S(2)}) async-start(), calls=%async_computation.2 | async-start | bytes 15138816 | tf_op jit(solution)/shard_map/all_gather | solution.py:31
  129.6 46.0 %all-to-all-start = ((f32[32,1,25600]{2,1,0:T(1,128)}), f32[32,1,25600]{2,1,0:T(1,128)}, u32[]{:S(2)}, u32[]{:S(2)}) async-start(f32[32,1,25600]{2,1,0:T(1,128)} %reshape.113), calls=%async_computation | async-start | bytes 6553600 | tf_op jit(solution)/shard_map/all_to_all | solution.py:42
  135.0 179.1 %all-reduce.2.cloned.1.call-start = ((), (), s32[]{:S(2)}) async-start(), calls=%async_computation.1 | async-start | bytes 6553600 | tf_op jit(solution)/shard_map/psum | solution.py:44
  236.6 0.7 copy-start.4
  236.6 0.7 copy-start.3
  236.6 77.5 %copy-start.1 = (bf16[10,40,512]{2,1,0:T(8,128)(2,1)S(1)}, bf16[10,40,512]{2,1,0:T(8,128)(2,1)}, u32[]{:S(2)}) copy-start(bf16[10,40,512]{2,1,0:T(8,128)(2,1)} %param.11) | copy-start | bytes 1228804
Sparse Core Ops, SparseCore 0:
  9.6 71.2 all-gather.2
  236.7 77.3 all-reduce.1
where the time goes:
time: 324 us; the launch traced here: 323 us
  waiting for transfers between devices  151 us (47%)
  local copies, waits for them, and re-layouts  112 us (35%)
  other arithmetic  21 us (6%)
  matrix products  19.4 us (6%)
  between operations  13.5 us (4%)
  starting transfers between devices  5.5 us (2%)
    psum x1, waiting for transfers between devices, shards(): totals = lax.psum(((ladder + direct + mirror,)[0],), 'rep')  76.6 us
    all_gather x1, waiting for transfers between devices, shards(): gathered = lax.all_gather(screened, 'pair', axis=0, tiled=True)  65.9 us
    unnamed x15, local copies, waits for them, and re-layouts  49.6 us
    reshape x1, local copies, waits for them, and re-layouts, shards(): gathered.reshape(occ, occ, c_loc, virt)  18.2 us
    dot_general x1, matrix products, shards(): jnp.dot(gathered, ladder_ints, preferred_element_type=jnp.float32)  12.4 us
    all_to_all x1, other arithmetic, shards(): lax.all_to_all(cycle_tr, 'pair', split_axis=3, concat_axis=2, tiled=True)  12 us
    all_to_all x3, local copies, waits for them, and re-layouts, shards(): lax.all_to_all(cycle_tr, 'pair', split_axis=3, concat_axis=2, tiled=True)  10.2 us
    transpose x1, local copies, waits for them, and re-layouts, shards(): mirror = jnp.transpose(swapped, (0, 1, 3, 2)).reshape(occ, occ, ab_loc)  9.34 us
  transfers between devices with their start and end apart: 3, of which 3 were waited for; matrix products, arithmetic and copies ran while one was open for 12% of the time, Pallas kernels for 0%

commit v1 on v0

v1 whole, which is shorter than its diff:
```python
import jax
import jax.numpy as jnp
from jax import lax
from jax.experimental import pallas as pl
from jax.experimental.pallas import tpu as pltpu
from jax.sharding import PartitionSpec as P

NG = 5
NM = 8
NK = 40
ROWS = 10
NC = 32
F32 = jnp.float32
BF16 = jnp.bfloat16
MESH = pl.DeviceIdType.MESH


def kernel(
    amp_ref, mask_ref, v_hbm, w_ref, lbar_ref, xbar_ref,
    s, v, tmp, s2, lad, cyc, lad_far, cyc_far, lad_in, cyc_in,
    v_sem, send_s, recv_f, recv_g, recv_b, send_r, recv_far, recv_in,
):
    p = lax.axis_index("pair")
    r = lax.axis_index("rep")
    h = p % 2
    x = (p // 2) % 4
    y = p // 8
    f = x + h * (y - x)
    gg = y + h * (x - y)
    sf = 1 + 3 * h
    sg = 4 - 3 * h

    def blk(df, dg):
        return 2 * (((f + df) % 4) * sf + ((gg + dg) % 4) * sg) + h

    sib = p + 1 - 2 * h
    fp, fm, gp, gm = blk(1, 0), blk(3, 0), blk(0, 1), blk(0, 3)
    up, down, far = (r + 1) % 4, (r + 3) % 4, (r + 2) % 4

    pltpu.make_async_copy(v_hbm, v, v_sem).start()

    barrier = pltpu.get_barrier_semaphore()
    for q in (fp, fm, gp, gm, sib):
        pl.semaphore_signal(barrier, inc=1, device_id=(q, r), device_id_type=MESH)
    for q in (up, down):
        pl.semaphore_signal(barrier, inc=1, device_id=(p, q), device_id_type=MESH)

    for c in range(NC):
        piece = amp_ref[:, c * 128 : (c + 1) * 128].astype(F32) * mask_ref[...]
        tmp[pl.ds(c, 50, stride=NC), :] = piece
    for n in range(50):
        s[n % NG, p, n // NG] = tmp[n * NC : (n + 1) * NC, :].astype(BF16)

    pl.semaphore_wait(barrier, 7)

    def send(src, dst, ssem, rsem, dev):
        pltpu.make_async_remote_copy(
            src_ref=src, dst_ref=dst, send_sem=ssem, recv_sem=rsem, device_id=dev, device_id_type=MESH
        ).start()

    def wait(ref, sem):
        pltpu.make_async_copy(ref, ref, sem).wait()

    def whole(g, b, sem, to):
        send(s.at[g, b], s.at[g, b], send_s.at[g], sem, (to, r))

    def half(g, b, at, sem, to):
        send(s.at[g, b, pl.ds(at, 5)], s.at[g, b, pl.ds(at, 5)], send_s.at[g], sem, (to, r))

    offs = (0, 3, 1, 2)

    def start_own(g):
        whole(g, p, recv_f.at[g, 0], fp)
        whole(g, p, recv_f.at[g, 1], fm)
        start_g(g, 0)

    def start_g(g, col):
        b = blk(offs[col], 0)
        whole(g, b, recv_g.at[g, col, 0], gp)
        whole(g, b, recv_g.at[g, col, 1], gm)
        whole(g, b, recv_b.at[g, col], sib)

    def pass_f(g):
        wait(s.at[g, 0], recv_f.at[g, 0])
        half(g, fm, 0, recv_f.at[g, 2], fp)
        start_g(g, 1)
        wait(s.at[g, 0], recv_f.at[g, 1])
        half(g, fp, 5, recv_f.at[g, 2], fm)
        start_g(g, 2)

    def last_f(g):
        wait(s.at[g, 0], recv_f.at[g, 2])
        start_g(g, 3)

    def pass_g(g, col):
        below, above = blk(offs[col], 3), blk(offs[col], 1)
        wait(s.at[g, 0], recv_g.at[g, col, 0])
        half(g, below, 0, recv_g.at[g, col, 2], gp)
        whole(g, below, recv_b.at[g, col], sib)
        wait(s.at[g, 0], recv_g.at[g, col, 1])
        half(g, above, 5, recv_g.at[g, col, 2], gm)
        whole(g, above, recv_b.at[g, col], sib)

    def last_g(g, col):
        wait(s.at[g, 0], recv_g.at[g, col, 2])
        whole(g, blk(offs[col], 2), recv_b.at[g, col], sib)

    def quarter(g, n):
        if n % 2 == 0:
            c0 = 16 * (n // 2)

            def widen(b, _):
                for u in range(ROWS):
                    tmp[pl.ds(pl.multiple_of((b * ROWS + u) * 16, 16), 16), :] = s[g, b, u, c0 : c0 + 16, :].astype(F32)
                return 0

            lax.fori_loop(0, 32, widen, 0)
        for c in range(8):
            s2[:, c * 128 : (c + 1) * 128] = tmp[pl.ds(8 * (n % 2) + c, 320, stride=16), :].astype(BF16)
        part = jnp.dot(s2[...], v[n * 1024 : (n + 1) * 1024, :], preferred_element_type=F32)
        for a in range(4):
            if n == 0:
                lad[g, a] = part[:, a * 128 : (a + 1) * 128]
            else:
                lad[g, a] += part[:, a * 128 : (a + 1) * 128]
        rows = []
        for k in range(NK):
            b0, u0 = divmod(NM * k + 2 * n, ROWS)
            b1, u1 = divmod(NM * k + 2 * n + 1, ROWS)
            rows.append(jnp.concatenate([s[g, b0, u0], s[g, b1, u1]], axis=1))
        got = jnp.dot(w_ref[...], jnp.concatenate(rows, axis=0), preferred_element_type=F32)
        cyc[g, n] = got
        for m in range(2):
            for a in range(4):
                lad[g, a, pl.ds(2 * n + m, NK, stride=NM), :] += got[
                    a * NK : (a + 1) * NK, m * 128 : (m + 1) * 128
                ]

    def rows_of(t):
        return pl.ds(pl.multiple_of(t * 80, 80), 80)

    def reduce_1(g):
        send(lad.at[g, :, rows_of(far)], lad_far.at[g], send_r.at[g, 0], recv_far.at[g, 0], (p, up))
        send(cyc.at[g, far], cyc_far.at[g], send_r.at[g, 1], recv_far.at[g, 1], (p, down))
        send(cyc.at[g, up], cyc_in.at[g, 0], send_r.at[g, 2], recv_in.at[g, 0], (p, up))
        send(lad.at[g, :, rows_of(down)], lad_in.at[g, 1], send_r.at[g, 3], recv_in.at[g, 1], (p, down))

    def reduce_2(g):
        wait(lad_far.at[g], recv_far.at[g, 0])
        lad[g, :, rows_of(up), :] += lad_far[g]
        send(lad.at[g, :, rows_of(up)], lad_in.at[g, 0], send_r.at[g, 4], recv_in.at[g, 2], (p, up))
        wait(cyc_far.at[g], recv_far.at[g, 1])
        cyc[g, down] += cyc_far[g]
        send(cyc.at[g, down], cyc_in.at[g, 1], send_r.at[g, 5], recv_in.at[g, 3], (p, down))

    def reduce_3(g):
        wait(cyc_in.at[g, 0], recv_in.at[g, 0])
        wait(lad_in.at[g, 1], recv_in.at[g, 1])
        wait(lad_in.at[g, 0], recv_in.at[g, 2])
        wait(cyc_in.at[g, 1], recv_in.at[g, 3])
        xbar_ref[g] = cyc[g, r] + cyc_in[g, 0] + cyc_in[g, 1]
        total = lad[g, :, rows_of(r), :] + lad_in[g, 0] + lad_in[g, 1]
        for i in range(10):
            for a in range(4):
                lbar_ref[a, pl.ds(i * NK + g, NM, stride=NG), :] = total[a, i * NM : (i + 1) * NM, :]

    start_own(0)
    wait(v, v_sem)

    def step(it, _):
        on, back = it < NG, it >= 1
        done = it - 1
        pl.when(on)(lambda: pass_f(it))
        pl.when(back)(lambda: quarter(done, 0))

        @pl.when(on)
        def _():
            pass_g(it, 0)
            last_f(it)

        pl.when(back)(lambda: quarter(done, 1))
        pl.when(it >= 2)(lambda: reduce_2(it - 2))

        @pl.when(on)
        def _():
            pass_g(it, 1)
            pass_g(it, 2)

        pl.when(it + 1 < NG)(lambda: start_own(it + 1))
        pl.when(back)(lambda: quarter(done, 2))

        @pl.when(on)
        def _():
            last_g(it, 0)
            last_g(it, 1)
            pass_g(it, 3)

        @pl.when(back)
        def _():
            quarter(done, 3)
            reduce_1(done)

        @pl.when(on)
        def _():
            last_g(it, 2)
            last_g(it, 3)
            for col in range(4):
                wait(s.at[it, pl.ds(0, 4)], recv_b.at[it, col])

        return 0

    lax.fori_loop(0, NG + 1, step, 0)
    reduce_2(NG - 1)

    def finish(g, _):
        reduce_3(g)
        wait(s.at[g, pl.ds(0, 31)], send_s.at[g])
        for n in range(6):
            if n in (0, 3, 4):
                wait(lad_far.at[g], send_r.at[g, n])
            else:
                wait(cyc_far.at[g], send_r.at[g, n])
        return 0

    lax.fori_loop(0, NG, finish, 0)


def fused(amp, mask, v, w):
    vmem = pl.BlockSpec(memory_space=pltpu.VMEM)
    dma = pltpu.SemaphoreType.DMA
    return pl.pallas_call(
        kernel,
        out_shape=(
            jax.ShapeDtypeStruct((4, 400, 128), F32),
            jax.ShapeDtypeStruct((NG, 160, 256), F32),
        ),
        in_specs=[vmem, vmem, pl.BlockSpec(memory_space=pl.ANY), vmem],
        out_specs=(vmem, vmem),
        scratch_shapes=[
            pltpu.VMEM((NG, 32, ROWS, NC, 128), BF16),
            pltpu.VMEM((4096, 512), BF16),
            pltpu.VMEM((320 * 16, 128), F32),
            pltpu.VMEM((320, 1024), BF16),
            pltpu.VMEM((NG, 4, 320, 128), F32),
            pltpu.VMEM((NG, 4, 160, 256), F32),
            pltpu.VMEM((NG, 4, 80, 128), F32),
            pltpu.VMEM((NG, 160, 256), F32),
            pltpu.VMEM((NG, 2, 4, 80, 128), F32),
            pltpu.VMEM((NG, 2, 160, 256), F32),
            dma,
            dma((NG,)),
            dma((NG, 3)),
            dma((NG, 4, 3)),
            dma((NG, 4)),
            dma((NG, 6)),
            dma((NG, 2)),
            dma((NG, 4)),
        ],
        compiler_params=pltpu.CompilerParams(
            collective_id=0, has_side_effects=True, vmem_limit_bytes=60 * 1024 * 1024
        ),
    )(amp, mask, v, w)


def shards(amplitude, tile_mask, ladder_ints, cycle_ints, coulomb, eps_occ, eps_vir):
    pair_at = lax.axis_index("pair")
    rep_at = lax.axis_index("rep")
    rows = lax.dynamic_slice(tile_mask.reshape(1600, 2, 2), (pair_at * 50, rep_at // 2, 0), (50, 1, 2))
    mask = jnp.repeat(rows.reshape(50, 2).astype(F32), 64, axis=1)
    w = cycle_ints.reshape(160, NC, NK).swapaxes(1, 2).reshape(160, NK * NC)
    lbar, xbar = fused(amplitude, mask, ladder_ints, w)
    swapped = lax.all_to_all(xbar.reshape(NG, 4, 40, 2, 32, 4), "pair", split_axis=4, concat_axis=4, tiled=True)
    mirror = jnp.transpose(swapped, (3, 0, 2, 5, 4, 1)).reshape(10, 40, 512)
    occ_mine = lax.dynamic_slice_in_dim(eps_occ, rep_at * 10, 10, 0)
    vir_first = lax.dynamic_slice_in_dim(eps_vir, pair_at * 4, 4, 0)
    vir_pairs = (vir_first[:, None] + eps_vir[None, :]).reshape(512)
    denom = vir_pairs[None, None, :] - occ_mine[:, None, None] - eps_occ[None, :, None]
    residual = coulomb.astype(F32) + lbar.swapaxes(0, 1).reshape(10, 40, 512) + mirror
    return (residual / denom).astype(BF16)


def solution(mesh):
    placed = (
        P("pair", "rep"),
        P(),
        P("rep", "pair"),
        P("pair", None, "rep"),
        P("rep", None, "pair"),
        P(),
        P(),
    )
    return jax.shard_map(
        shards, mesh=mesh, in_specs=placed, out_specs=P("rep", None, "pair"), check_vma=False
    )
```

time: 324 us -> 154 us (0.48)
  waiting for transfers between devices: 151 us -> 13.6 us
  Pallas kernels: 0 us -> 97.6 us
  local copies, waits for them, and re-layouts: 112 us -> 31.2 us
  matrix products: 19.4 us -> 0 us
  other arithmetic: 21 us -> 6.15 us
  between operations: 13.5 us -> 0.13 us
    pallas_call x0 -> x1, Pallas kernels: none -> 97.6 us  [fused(): pl.pallas_call(kernel, out_shape=(jax.ShapeDtypeStruct((4, 400, 128), F32...]
    psum x1 -> x0, waiting for transfers between devices: 76.6 us -> none  [shards(): totals = lax.psum(((ladder + direct + mirror,)[0],), 'rep')]
    all_gather x1 -> x0, waiting for transfers between devices: 65.9 us -> none  [shards(): gathered = lax.all_gather(screened, 'pair', axis=0, tiled=True)]
    unnamed x15 -> x9, local copies, waits for them, and re-layouts: 49.6 us -> 12.1 us
    reshape x7 -> x8, local copies, waits for them, and re-layouts: 33.5 us -> 12.2 us  [the longest x2 5.01 us: shards(): xbar.reshape(NG, 4, 40, 2, 32, 4)]
    dot_general x4 -> x0, matrix products: 19.4 us -> none  [the longest x1 12.4 us: shards(): jnp.dot(gathered, ladder_ints, preferred_element_type=jnp.float32)]
    transpose x3 -> x4, local copies, waits for them, and re-layouts: 18.8 us -> 3.39 us  [the longest x1 1.79 us: shards(): w = cycle_ints.reshape(160, NC, NK).swapaxes(1, 2).reshape(160, NK * NC)]
    all_to_all x3 -> x1, local copies, waits for them, and re-layouts: 10.2 us -> 0.51 us  [shards(): lax.all_to_all(xbar.reshape(NG, 4, 40, 2, 32, 4), 'pair', split_axis=4, c...]
  transfers between devices with their start and end apart: 3 -> 1, of which waited for: 3 -> 1; matrix products, arithmetic and copies ran while one was open for 12% -> 1% of each run, Pallas kernels for 0% -> 0%
where the time goes in v1:
time: 154 us; the launch traced here: 153 us
  Pallas kernels  97.6 us (63%)
  local copies, waits for them, and re-layouts  31.2 us (20%)
  waiting for transfers between devices  13.6 us (9%)
  other arithmetic  6.15 us (4%)
  starting transfers between devices  4.54 us (3%)
    pallas_call x1, Pallas kernels, fused(): pl.pallas_call(kernel, out_shape=(jax.ShapeDtypeStruct((4, 400, 128), F32...  97.6 us
    all_to_all x1, waiting for transfers between devices, shards(): lax.all_to_all(xbar.reshape(NG, 4, 40, 2, 32, 4), 'pair', split_axis=4, c...  13.6 us
    unnamed x9, local copies, waits for them, and re-layouts  12.1 us
    reshape x2, local copies, waits for them, and re-layouts, shards(): xbar.reshape(NG, 4, 40, 2, 32, 4)  5.01 us
    all_to_all x1, starting transfers between devices, shards(): lax.all_to_all(xbar.reshape(NG, 4, 40, 2, 32, 4), 'pair', split_axis=4, c...  4.54 us
    reshape x2, local copies, waits for them, and re-layouts, shards(): w = cycle_ints.reshape(160, NC, NK).swapaxes(1, 2).reshape(160, NK * NC)  4.29 us
    all_to_all x1, other arithmetic, shards(): lax.all_to_all(xbar.reshape(NG, 4, 40, 2, 32, 4), 'pair', split_axis=4, c...  3.64 us
  transfers between devices with their start and end apart: 1, of which 1 were waited for; matrix products, arithmetic and copies ran while one was open for 1% of the time, Pallas kernels for 0%

profile of v1, /device:TPU:1, one launch (start us, length us, event | category | flops | bytes accessed | tf_op | source)
XLA Modules:
  0.0 153.1 jit_solution(6536759168845381231)
XLA Ops:
  0.0 0.9 copy.19
  0.9 0.1 reshape.69
  1.0 0.1 convert_bitcast_fusion
  1.1 0.1 copy.20
  1.2 0.1 broadcast_in_dim.2
  1.3 0.7 reshape.70.mask_ref
  2.0 3.3 %reshape.71 = bf16[160,32,40]{2,1,0:T(8,128)(2,1)S(1)} reshape(bf16[4,40,1280]{2,1,0:T(8,128)(2,1)} %param.10) | data formatting | bytes 819200 | tf_op jit(solution)/shard_map/reshape | solution.py:270
  5.4 1.8 %copy.21 = bf16[160,40,32]{0,2,1:T(8,128)(2,1)S(1)} copy(bf16[160,40,32]{1,2,0:T(8,128)(2,1)S(1)} %bitcast.23) | data formatting | bytes 819200 | tf_op jit(solution)/shard_map/transpose | solution.py:270
  7.1 1.0 copy.22.w_ref
  8.1 97.6 %shard_map.73 = (f32[4,400,128]{2,1,0:T(8,128)}, f32[5,160,256]{2,1,0:T(8,128)}) custom-call(bf16[50,4096]{1,0:T(8,128)(2,1)} %amp_ref.1, f32[50,128]{1,0:T(8,128)} %reshape.70.mask_ref, bf16[4096,512]{1,0:T(8,128)(2,1)} %v_hbm.1, bf16[160,1280]{1,0:T(8,128)(2,1)} %copy.22.w_ref), custom_call_target="tpu_custom_call" | custom-call | tf_op jit(solution)/shard_map/pallas_call | solution.py:231
  105.7 2.6 %copy.24 = f32[5,160,256]{1,2,0:T(8,128)} copy(f32[5,160,256]{2,1,0:T(8,128)} %get-tuple-element.8) | data formatting | bytes 1638400 | tf_op jit(solution)/shard_map/pallas_call | solution.py:231
  108.3 2.6 %reshape.74 = f32[5,4,40,2,32,4]{2,1,5,4,3,0:T(4,128)S(1)} reshape(f32[5,160,256]{1,2,0:T(8,128)} %copy.24) | data formatting | bytes 1638400 | tf_op jit(solution)/shard_map/reshape | solution.py:272
  110.9 2.4 %copy.29 = f32[5,4,40,2,32,4]{2,1,5,3,0,4:T(4,128)} copy(f32[5,4,40,2,32,4]{2,1,5,4,3,0:T(4,128)S(1)} %reshape.74) | data formatting | bytes 1638400 | tf_op jit(solution)/shard_map/reshape | solution.py:272
  113.3 6.2 %reshape.76 = f32[32,1,6400]{2,1,0:T(1,128)} reshape(f32[32,5,2,4,4,40]{5,4,3,2,1,0:T(4,128)} %bitcast.21) | data formatting | bytes 1638400
  119.6 4.5 %all-to-all-start = ((f32[32,1,6400]{2,1,0:T(1,128)}), f32[32,1,6400]{2,1,0:T(1,128)S(1)}, u32[]{:S(2)}, u32[]{:S(2)}) async-start(f32[32,1,6400]{2,1,0:T(1,128)} %reshape.76), calls=%async_computation | async-start | bytes 1638400 | tf_op jit(solution)/shard_map/all_to_all | solution.py:272
  124.1 0.0 copy-done
  124.1 0.3 copy.23
  124.4 0.3 reshape.73
  124.8 0.0 copy-done.2
  124.8 0.1 dynamic_slice.11
  124.9 0.0 copy-done.1
  124.9 0.1 dynamic_slice.10
  125.0 0.1 add_bitcast_fusion
  125.0 0.1 broadcast_subtract_fusion
  125.1 13.6 %all-to-all-done = f32[32,1,6400]{2,1,0:T(1,128)S(1)} async-done(((f32[32,1,6400]{2,1,0:T(1,128)}), f32[32,1,6400]{2,1,0:T(1,128)S(1)}, u32[]{:S(2)}, u32[]{:S(2)}) %all-to-all-start) | async-done | bytes 819232 | tf_op jit(solution)/shard_map/all_to_all | solution.py:272
  138.7 0.5 broadcast.26
  139.2 3.6 %reduce = f32[32,6400]{1,0:T(8,128)} reduce(f32[32,1,6400]{2,1,0:T(1,128)S(1)} %all-to-all-done, f32[]{:T(128)} %broadcast.26), dimensions={1}, to_apply=%all_to_all.3.reduce_sub_computation | reduce | bytes 1638404 | tf_op jit(solution)/shard_map/all_to_all | solution.py:272
  142.8 5.0 %reshape.77 = f32[32,5,2,4,4,40]{5,4,3,2,1,0:T(4,128)S(1)} reshape(f32[32,6400]{1,0:T(8,128)} %reduce) | data formatting | bytes 1638400
  147.8 0.6 bitcast_bitcast_fusion
  148.4 0.7 copy.26
  149.1 1.7 %copy.27 = f32[10,40,512]{2,1,0:T(8,128)} copy(f32[10,40,512]{1,2,0:T(8,128)S(1)} %bitcast.22) | data formatting | bytes 1638400 | tf_op jit(solution)/shard_map/reshape | solution.py:273
  150.9 2.3 %divide_convert_fusion = bf16[10,40,512]{2,1,0:T(8,128)(2,1)} fusion(f32[10,40,512]{2,1,0:T(8,128)} %copy.27, f32[10,40,512]{2,1,0:T(8,128)S(1)} %reshape.73, bf16[10,40,512]{2,1,0:T(8,128)(2,1)} %param.11, f32[40]{0:T(128)S(1)} %copy-done.2, f32[10,512]{1,0:T(8,128)S(1)} %broadcast_subtract_fusion), kind=kLoop, calls=%fused_computation | loop fusion | flops 1228800 | bytes 2478240 | tf_op jit(solution)/shard_map/convert_element_type | solution.py:279
  (3 shorter events, 0.0 us)
Async XLA Ops:
  113.3 10.8 %copy-start = (f32[4,400,128]{2,1,0:T(8,128)S(1)}, f32[4,400,128]{2,1,0:T(8,128)}, u32[]{:S(2)}) copy-start(f32[4,400,128]{2,1,0:T(8,128)} %get-tuple-element.7) | copy-start | bytes 2457604
  119.6 5.2 %copy-start.2 = (f32[40]{0:T(128)S(1)}, f32[40]{0:T(128)}, u32[]{:S(2)}) copy-start(f32[40]{0:T(128)} %param.12) | copy-start | bytes 484
  119.6 5.3 %copy-start.1 = (f32[128]{0:T(128)S(1)}, f32[128]{0:T(128)}, u32[]{:S(2)}) copy-start(f32[128]{0:T(128)} %param.13) | copy-start | bytes 1540
  119.6 19.1 %all-to-all-start = ((f32[32,1,6400]{2,1,0:T(1,128)}), f32[32,1,6400]{2,1,0:T(1,128)S(1)}, u32[]{:S(2)}, u32[]{:S(2)}) async-start(f32[32,1,6400]{2,1,0:T(1,128)} %reshape.76), calls=%async_computation | async-start | bytes 1638400 | tf_op jit(solution)/shard_map/all_to_all | solution.py:272

commit v2 on v1

v2 whole, which is shorter than its diff:
```python
import jax
import jax.numpy as jnp
from jax import lax
from jax.experimental import pallas as pl
from jax.experimental.pallas import tpu as pltpu
from jax.sharding import PartitionSpec as P

NG = 5
NM = 8
NK = 40
STEPS = 32512.0
ROWS = 10
NC = 32
F32 = jnp.float32
BF16 = jnp.bfloat16
MESH = pl.DeviceIdType.MESH


def encode(dst, val):
    size = jnp.maximum(jnp.max(jnp.abs(val), axis=0, keepdims=True), 1e-30)
    log = jnp.ceil(jnp.log(size) * 128.0)
    dst[0:320] = jnp.round(val * (jnp.exp(log * (-1 / 128)) * STEPS)).astype(jnp.int32).astype(jnp.int16)
    dst[320:336] = jnp.broadcast_to(log, (16, 128)).astype(jnp.int32).astype(jnp.int16)


def decode(src):
    log = src[320:336].astype(jnp.int32).astype(F32)[0:1]
    return src[0:320].astype(jnp.int32).astype(F32) * (jnp.exp(log * (1 / 128)) * (1 / STEPS))


def kernel(
    amp_ref, mask_ref, v_hbm, w_ref, coul_ref, occ_ref, vir_ref, occ_smem, vir_smem, out_ref,
    s, v, wnat, wp, tmp, s2, lad, cyc, red_out, red_in, msg, z, msg_out, msg_in, fin, mir,
    v_sem, send_s, recv_f, recv_g, recv_b, send_r, recv_r, send_m, recv_m,
):
    p = lax.axis_index("pair")
    r = lax.axis_index("rep")
    h = p % 2
    x = (p // 2) % 4
    y = p // 8
    f = x + h * (y - x)
    gg = y + h * (x - y)
    sf = 1 + 3 * h
    sg = 4 - 3 * h

    def blk(df, dg):
        return 2 * (((f + df) % 4) * sf + ((gg + dg) % 4) * sg) + h

    sib = p + 1 - 2 * h
    fp, fm, gp, gm = blk(1, 0), blk(3, 0), blk(0, 1), blk(0, 3)
    up, down, far = (r + 1) % 4, (r + 3) % 4, (r + 2) % 4

    pltpu.make_async_copy(v_hbm, v, v_sem).start()

    barrier = pltpu.get_barrier_semaphore()

    @pl.loop(1, 32)
    def _(n):
        pl.semaphore_signal(barrier, inc=1, device_id=((p + n) % 32, r), device_id_type=MESH)

    for q in (up, down):
        pl.semaphore_signal(barrier, inc=1, device_id=(p, q), device_id_type=MESH)

    for c in range(NC):
        piece = amp_ref[:, c * 128 : (c + 1) * 128].astype(F32) * mask_ref[...]
        tmp[pl.ds(c, 50, stride=NC), :] = piece
    for n in range(50):
        s[n % NG, p, n // NG] = tmp[n * NC : (n + 1) * NC, :].astype(BF16)

    pl.semaphore_wait(barrier, 33)

    def send(src, dst, ssem, rsem, dev):
        pltpu.make_async_remote_copy(
            src_ref=src, dst_ref=dst, send_sem=ssem, recv_sem=rsem, device_id=dev, device_id_type=MESH
        ).start()

    def wait(ref, sem):
        pltpu.make_async_copy(ref, ref, sem).wait()

    def whole(g, b, sem, to):
        send(s.at[g, b], s.at[g, b], send_s.at[g], sem, (to, r))

    def half(g, b, at, sem, to):
        send(s.at[g, b, pl.ds(at, 5)], s.at[g, b, pl.ds(at, 5)], send_s.at[g], sem, (to, r))

    offs = (0, 3, 1, 2)

    def start_f(g):
        whole(g, p, recv_f.at[g, 0], fp)
        whole(g, p, recv_f.at[g, 1], fm)

    def start_g(g, col):
        b = blk(offs[col], 0)
        whole(g, b, recv_g.at[g, col, 0], gp)
        whole(g, b, recv_g.at[g, col, 1], gm)
        whole(g, b, recv_b.at[g, col], sib)

    def pass_f(g):
        wait(s.at[g, 0], recv_f.at[g, 0])
        half(g, fm, 0, recv_f.at[g, 2], fp)
        wait(s.at[g, 0], recv_f.at[g, 1])
        half(g, fp, 5, recv_f.at[g, 2], fm)

    def last_f(g):
        wait(s.at[g, 0], recv_f.at[g, 2])

    def pass_g(g, col):
        below, above = blk(offs[col], 3), blk(offs[col], 1)
        wait(s.at[g, 0], recv_g.at[g, col, 0])
        half(g, below, 0, recv_g.at[g, col, 2], gp)
        whole(g, below, recv_b.at[g, col], sib)
        wait(s.at[g, 0], recv_g.at[g, col, 1])
        half(g, above, 5, recv_g.at[g, col, 2], gm)
        whole(g, above, recv_b.at[g, col], sib)

    def last_g(g, col):
        wait(s.at[g, 0], recv_g.at[g, col, 2])
        whole(g, blk(offs[col], 2), recv_b.at[g, col], sib)

    def sort_w():
        for a in range(4):
            wnat[a * NK : (a + 1) * NK, :] = w_ref[a].astype(F32)
        total = jnp.zeros((160, 1280), F32)
        for n in range(5):
            row = n * 256 + lax.broadcasted_iota(jnp.int32, (256, 1280), 0)
            col = lax.broadcasted_iota(jnp.int32, (256, 1280), 1)
            perm = (row == (col & 31) * NK + (col >> 5)).astype(F32).astype(BF16)
            total += jnp.dot(wnat[:, n * 256 : (n + 1) * 256].astype(BF16), perm, preferred_element_type=F32)
        wp[...] = total.astype(BF16)

    def quarter(g, n):
        if n % 2 == 0:
            c0 = 16 * (n // 2)

            def widen(b, _):
                for u in range(ROWS):
                    tmp[pl.ds(pl.multiple_of((b * ROWS + u) * 16, 16), 16), :] = s[g, b, u, c0 : c0 + 16, :].astype(F32)
                return 0

            lax.fori_loop(0, 32, widen, 0)
        for c in range(8):
            s2[:, c * 128 : (c + 1) * 128] = tmp[pl.ds(8 * (n % 2) + c, 320, stride=16), :].astype(BF16)
        part = jnp.dot(s2[...], v[n * 1024 : (n + 1) * 1024, :], preferred_element_type=F32)
        for a in range(4):
            if n == 0:
                lad[g, a] = part[:, a * 128 : (a + 1) * 128]
            else:
                lad[g, a] += part[:, a * 128 : (a + 1) * 128]
        rows = []
        for k in range(NK):
            b0, u0 = divmod(NM * k + 2 * n, ROWS)
            b1, u1 = divmod(NM * k + 2 * n + 1, ROWS)
            rows.append(jnp.concatenate([s[g, b0, u0], s[g, b1, u1]], axis=1))
        got = jnp.dot(wp[...], jnp.concatenate(rows, axis=0), preferred_element_type=F32)
        cyc[g, n, 0] = got[:, 0:128]
        cyc[g, n, 1] = got[:, 128:256]
        for m in range(2):
            for a in range(4):
                lad[g, a, pl.ds(2 * n + m, NK, stride=NM), :] += got[
                    a * NK : (a + 1) * NK, m * 128 : (m + 1) * 128
                ]

    def rows_of(t):
        return pl.ds(pl.multiple_of(t * 80, 80), 80)

    def lad_of(g, t):
        return lad[g, :, rows_of(t), :].reshape(320, 128)

    def cyc_of(g, t):
        return cyc[g, t].reshape(320, 128)

    def ship(g, n, val, to):
        encode(red_out.at[g, n], val)
        send(red_out.at[g, n], red_in.at[g, n], send_r.at[g], recv_r.at[g, n], (p, to))

    def take(g, n):
        wait(red_in.at[g, n], recv_r.at[g, n])
        return decode(red_in.at[g, n])

    def reduce_1(g):
        ship(g, 0, lad_of(g, far), up)
        ship(g, 2, cyc_of(g, far), down)
        ship(g, 1, cyc_of(g, up), up)
        ship(g, 3, lad_of(g, down), down)

    def reduce_2(g):
        ship(g, 4, lad_of(g, up) + take(g, 0), up)
        ship(g, 5, cyc_of(g, down) + take(g, 2), down)

    def reduce_3(g):
        whole_cyc = (cyc_of(g, r) + take(g, 1) + take(g, 5)).reshape(2, 160, 128)
        for b in range(4):
            val = whole_cyc[:, b * NK : (b + 1) * NK, :].reshape(80, 128)
            size = jnp.maximum(jnp.max(jnp.abs(val), axis=0, keepdims=True), 1e-30)
            log = jnp.ceil(jnp.log(size) * 128.0)
            code = jnp.round(val * (jnp.exp(log * (-1 / 128)) * STEPS))
            msg[pl.ds(b, 128, stride=4), :] = jnp.concatenate([code, jnp.broadcast_to(log, (48, 128))], axis=0).T
        msg_out[g] = msg[...].astype(jnp.int32).astype(jnp.int16).reshape(32, 16, 128)
        msg_in[g, p] = msg_out[g, p]
        total = (lad_of(g, r) + take(g, 3) + take(g, 4)).reshape(4, 80, 128)
        for i in range(10):
            for a in range(4):
                fin[a, pl.ds(i * NK + g, NM, stride=NG), :] = total[a, i * NM : (i + 1) * NM, :]

    batches = ((0, NG - 1), (NG - 1, 1))

    def exchange(n):
        at = pl.ds(*batches[n])

        @pl.loop(1, 32)
        def _(d):
            to = (p + d) % 32
            send(msg_out.at[at, to], msg_in.at[at, p], send_m.at[n], recv_m.at[n], (to, r))

    def exchanged(n):
        part = msg_in.at[pl.ds(*batches[n]), pl.ds(0, 31)]
        wait(part, recv_m.at[n])

    def mirror(g):
        msg[...] = msg_in[g].reshape(512, 128).astype(jnp.int32).astype(F32)
        for a in range(4):
            for b in range(4):
                z[a, pl.ds(b, 32, stride=4), :] = msg[pl.ds(a * 4 + b, 32, stride=16), :]
        for a in range(4):
            turned = z[a].T
            val = turned[0:80] * (jnp.exp(turned[80:81] * (1 / 128)) * (1 / STEPS))
            for m in range(2):
                mir[a, pl.ds(pl.multiple_of((NG * m + g) * NK, 8), NK), :] = val[m * NK : (m + 1) * NK]

    start_f(0)

    def step(it, _):
        new, old, done = it, it - 1, it - 2
        is_new, is_old, is_done = it < NG, (it >= 1) & (it <= NG), it >= 2

        @pl.when(is_new)
        def _():
            start_g(new, 0)

        @pl.when(is_old)
        def _():
            pass_g(old, 2)
            last_g(old, 0)

        @pl.when(is_done)
        def _():
            for col in range(4):
                wait(s.at[done, pl.ds(0, 4)], recv_b.at[done, col])
            quarter(done, 0)

        @pl.when(is_new)
        def _():
            pass_f(new)
            start_g(new, 1)

        @pl.when(it == 1)
        def _():
            sort_w()
            wait(v, v_sem)

        @pl.when(is_old)
        def _():
            pass_g(old, 3)
            last_g(old, 1)

        pl.when(is_done)(lambda: quarter(done, 1))
        pl.when(it >= 3)(lambda: reduce_2(it - 3))

        @pl.when(is_new)
        def _():
            pass_g(new, 0)
            start_g(new, 2)

        pl.when(is_old)(lambda: last_g(old, 2))
        pl.when(is_done)(lambda: quarter(done, 2))
        pl.when(it + 1 < NG)(lambda: start_f(it + 1))

        @pl.when(is_new)
        def _():
            last_f(new)
            start_g(new, 3)
            pass_g(new, 1)

        pl.when(is_old)(lambda: last_g(old, 3))

        @pl.when(is_done)
        def _():
            quarter(done, 3)
            reduce_1(done)

        pl.when(it >= 3)(lambda: reduce_3(it - 3))
        return 0

    lax.fori_loop(0, NG + 2, step, 0)
    exchange(0)
    reduce_2(NG - 1)
    reduce_3(NG - 1)
    exchange(1)
    exchanged(0)

    @pl.loop(0, NG - 1)
    def _(g):
        mirror(g)

    exchanged(1)
    mirror(NG - 1)

    @pl.loop(0, 10)
    def _(i):
        rows = pl.ds(pl.multiple_of(i * NK, 8), NK)
        for a in range(4):
            lanes = slice(a * 128, (a + 1) * 128)
            residual = coul_ref[i, :, lanes].astype(F32) + fin[a, rows, :] + mir[a, rows, :]
            denom = (vir_smem[p * 4 + a] + vir_ref[...]) - occ_smem[r * 10 + i] - occ_ref[...]
            out_ref[i, :, lanes] = (residual / denom).astype(BF16)

    for g in range(NG):
        wait(s.at[g, pl.ds(0, 31)], send_s.at[g])
        wait(red_out.at[g], send_r.at[g])
    for n in range(2):
        wait(msg_out.at[pl.ds(*batches[n]), pl.ds(0, 31)], send_m.at[n])


def fused(amp, mask, v, w, coulomb, eps_occ, eps_vir):
    vmem = pl.BlockSpec(memory_space=pltpu.VMEM)
    smem = pl.BlockSpec(memory_space=pltpu.SMEM)
    dma = pltpu.SemaphoreType.DMA
    return pl.pallas_call(
        kernel,
        out_shape=jax.ShapeDtypeStruct((10, NK, 512), BF16),
        in_specs=[vmem, vmem, pl.BlockSpec(memory_space=pl.ANY), vmem, vmem, vmem, vmem, smem, smem],
        out_specs=vmem,
        scratch_shapes=[
            pltpu.VMEM((NG, 32, ROWS, NC, 128), BF16),
            pltpu.VMEM((4096, 512), BF16),
            pltpu.VMEM((160, 1280), F32),
            pltpu.VMEM((160, 1280), BF16),
            pltpu.VMEM((320 * 16, 128), F32),
            pltpu.VMEM((320, 1024), BF16),
            pltpu.VMEM((NG, 4, 320, 128), F32),
            pltpu.VMEM((NG, 4, 2, 160, 128), F32),
            pltpu.VMEM((NG, 6, 336, 128), jnp.int16),
            pltpu.VMEM((NG, 6, 336, 128), jnp.int16),
            pltpu.VMEM((512, 128), F32),
            pltpu.VMEM((4, 128, 128), F32),
            pltpu.VMEM((NG, 32, 16, 128), jnp.int16),
            pltpu.VMEM((NG, 32, 16, 128), jnp.int16),
            pltpu.VMEM((4, 400, 128), F32),
            pltpu.VMEM((4, 400, 128), F32),
            dma,
            dma((NG,)),
            dma((NG, 3)),
            dma((NG, 4, 3)),
            dma((NG, 4)),
            dma((NG,)),
            dma((NG, 6)),
            dma((2,)),
            dma((2,)),
        ],
        compiler_params=pltpu.CompilerParams(
            collective_id=0, has_side_effects=True, vmem_limit_bytes=60 * 1024 * 1024
        ),
    )(amp, mask, v, w, coulomb, eps_occ.reshape(NK, 1), eps_vir.reshape(1, 128), eps_occ, eps_vir)


def shards(amplitude, tile_mask, ladder_ints, cycle_ints, coulomb, eps_occ, eps_vir):
    pair_at = lax.axis_index("pair")
    rep_at = lax.axis_index("rep")
    rows = lax.dynamic_slice(tile_mask.reshape(1600, 2, 2), (pair_at * 50, rep_at // 2, 0), (50, 1, 2))
    mask = jnp.repeat(rows.reshape(50, 2).astype(F32), 64, axis=1)
    return fused(amplitude, mask, ladder_ints, cycle_ints, coulomb, eps_occ, eps_vir)


def solution(mesh):
    placed = (
        P("pair", "rep"),
        P(),
        P("rep", "pair"),
        P("pair", None, "rep"),
        P("rep", None, "pair"),
        P(),
        P(),
    )
    return jax.shard_map(
        shards, mesh=mesh, in_specs=placed, out_specs=P("rep", None, "pair"), check_vma=False
    )
```

time: 154 us -> 87.6 us (0.57)
  local copies, waits for them, and re-layouts: 31.2 us -> 5.05 us
  Pallas kernels: 97.6 us -> 82.2 us
  waiting for transfers between devices: 13.6 us -> 0 us
  other arithmetic: 6.15 us -> 0.08 us
  starting transfers between devices: 4.54 us -> 0 us
    pallas_call x1, Pallas kernels: 97.6 us -> 82.2 us  [fused(): pl.pallas_call(kernel, out_shape=jax.ShapeDtypeStruct((10, NK, 512), BF16...]
    all_to_all x1 -> x0, waiting for transfers between devices: 13.6 us -> none  [shards(): lax.all_to_all(xbar.reshape(NG, 4, 40, 2, 32, 4), 'pair', split_axis=4, c...]
    reshape x6 -> x1, local copies, waits for them, and re-layouts: 11.4 us -> 1.34 us  [fused(): eps_occ.reshape(NK, 1)]
    unnamed x9 -> x2, local copies, waits for them, and re-layouts: 12.1 us -> 2.67 us
    all_to_all x1 -> x0, starting transfers between devices: 4.54 us -> none  [shards(): lax.all_to_all(xbar.reshape(NG, 4, 40, 2, 32, 4), 'pair', split_axis=4, c...]
    all_to_all x1 -> x0, other arithmetic: 3.64 us -> none  [shards(): lax.all_to_all(xbar.reshape(NG, 4, 40, 2, 32, 4), 'pair', split_axis=4, c...]
    transpose x4 -> x0, local copies, waits for them, and re-layouts: 3.39 us -> none  [the longest x1 1.79 us: shards(): w = cycle_ints.reshape(160, NC, NK).swapaxes(1, 2).reshape(160, NK * NC)]
    pallas_call x1 -> x0, local copies, waits for them, and re-layouts: 2.61 us -> none  [fused(): pl.pallas_call(kernel, out_shape=(jax.ShapeDtypeStruct((4, 400, 128), F32...]
  transfers between devices with their start and end apart: 1 -> 0, of which waited for: 1 -> 0; matrix products, arithmetic and copies ran while one was open for 1% -> 0% of each run, Pallas kernels for 0% -> 0%
where the time goes in v2:
time: 87.6 us; the launch traced here: 87.4 us
  Pallas kernels  82.2 us (94%)
  local copies, waits for them, and re-layouts  5.05 us (6%)
    pallas_call x1, Pallas kernels, fused(): pl.pallas_call(kernel, out_shape=jax.ShapeDtypeStruct((10, NK, 512), BF16...  82.2 us
    unnamed x2, local copies, waits for them, and re-layouts  2.67 us

profile of v2, /device:TPU:1, one launch (start us, length us, event | category | flops | bytes accessed | tf_op | source)
XLA Modules:
  0.0 87.4 jit_solution(7338512237987396931)
XLA Ops:
  0.0 1.3 %copy.12.occ_ref = f32[40,1]{1,0:T(8,128)} copy(f32[40,1]{0,1:T(1,128)} %bitcast.9) | data formatting | bytes 320 | tf_op jit(solution)/shard_map/reshape | solution.py:363
  1.3 0.9 %copy.10 = s32[40,40,2,2]{1,0,3,2:T(8,128)S(1)} copy(s32[40,40,2,2]{1,3,2,0:T(2,128)} %param.8) | data formatting | bytes 51200 | tf_op args[1]
  2.2 0.1 reshape.14
  2.3 0.1 convert_bitcast_fusion
  2.4 0.1 copy.11
  2.5 0.1 broadcast_in_dim.3
  2.7 0.7 reshape.15.mask_ref
  3.4 82.2 %shard_map.73 = bf16[10,40,512]{2,1,0:T(8,128)(2,1)} custom-call(bf16[50,4096]{1,0:T(8,128)(2,1)} %amp_ref.1, f32[50,128]{1,0:T(8,128)} %reshape.15.mask_ref, bf16[4096,512]{1,0:T(8,128)(2,1)} %v_hbm.1, bf16[4,40,1280]{2,1,0:T(8,128)(2,1)} %w_ref.1, bf16[10,40,512]{2,1,0:T(8,128)(2,1)} %coul_ref.1, f32[40,1]{1,0:T(8,128)} %copy.12.occ_ref, ...), custom_call_target="tpu_custom_call" | custom-call | tf_op jit(solution)/shard_map/pallas_call | solution.py:328
  85.6 1.8 %copy.14 = bf16[10,40,512]{2,1,0:T(8,128)(2,1)} copy(bf16[10,40,512]{2,1,0:T(8,128)(2,1)} %shard_map.73) | data formatting | bytes 819200

commit v3 on v2

--- a/solution.py
+++ b/solution.py
@@ -43,11 +43,11 @@
     sf = 1 + 3 * h
     sg = 4 - 3 * h
 
-    def blk(df, dg):
+    def dev(df, dg):
         return 2 * (((f + df) % 4) * sf + ((gg + dg) % 4) * sg) + h
 
     sib = p + 1 - 2 * h
-    fp, fm, gp, gm = blk(1, 0), blk(3, 0), blk(0, 1), blk(0, 3)
+    fp, fm, gp, gm = dev(1, 0), dev(3, 0), dev(0, 1), dev(0, 3)
     up, down, far = (r + 1) % 4, (r + 3) % 4, (r + 2) % 4
 
     pltpu.make_async_copy(v_hbm, v, v_sem).start()
@@ -64,9 +64,13 @@
     for c in range(NC):
         piece = amp_ref[:, c * 128 : (c + 1) * 128].astype(F32) * mask_ref[...]
         tmp[pl.ds(c, 50, stride=NC), :] = piece
-    for n in range(50):
-        s[n % NG, p, n // NG] = tmp[n * NC : (n + 1) * NC, :].astype(BF16)
-
+
+    def own(g):
+        for u in range(ROWS):
+            n = u * NG + g
+            s[g, h, f, gg, u] = tmp[n * NC : (n + 1) * NC, :].astype(BF16)
+
+    own(0)
     pl.semaphore_wait(barrier, 33)
 
     def send(src, dst, ssem, rsem, dev):
@@ -77,45 +81,42 @@
     def wait(ref, sem):
         pltpu.make_async_copy(ref, ref, sem).wait()
 
-    def whole(g, b, sem, to):
-        send(s.at[g, b], s.at[g, b], send_s.at[g], sem, (to, r))
-
-    def half(g, b, at, sem, to):
-        send(s.at[g, b, pl.ds(at, 5)], s.at[g, b, pl.ds(at, 5)], send_s.at[g], sem, (to, r))
-
-    offs = (0, 3, 1, 2)
+    def ship_s(g, at, sem, to):
+        send(s.at[(g, h) + at], s.at[(g, h) + at], send_s.at[g], sem, (to, r))
 
     def start_f(g):
-        whole(g, p, recv_f.at[g, 0], fp)
-        whole(g, p, recv_f.at[g, 1], fm)
-
-    def start_g(g, col):
-        b = blk(offs[col], 0)
-        whole(g, b, recv_g.at[g, col, 0], gp)
-        whole(g, b, recv_g.at[g, col, 1], gm)
-        whole(g, b, recv_b.at[g, col], sib)
+        ship_s(g, (f, gg), recv_f.at[g, 0], fp)
+        ship_s(g, (f, gg), recv_f.at[g, 1], fm)
 
     def pass_f(g):
-        wait(s.at[g, 0], recv_f.at[g, 0])
-        half(g, fm, 0, recv_f.at[g, 2], fp)
-        wait(s.at[g, 0], recv_f.at[g, 1])
-        half(g, fp, 5, recv_f.at[g, 2], fm)
+        wait(s.at[g, 0, 0, 0], recv_f.at[g, 0])
+        ship_s(g, ((f + 3) % 4, gg, pl.ds(0, 5)), recv_f.at[g, 2], fp)
+        wait(s.at[g, 0, 0, 0], recv_f.at[g, 1])
+        ship_s(g, ((f + 1) % 4, gg, pl.ds(5, 5)), recv_f.at[g, 2], fm)
 
     def last_f(g):
-        wait(s.at[g, 0], recv_f.at[g, 2])
-
-    def pass_g(g, col):
-        below, above = blk(offs[col], 3), blk(offs[col], 1)
-        wait(s.at[g, 0], recv_g.at[g, col, 0])
-        half(g, below, 0, recv_g.at[g, col, 2], gp)
-        whole(g, below, recv_b.at[g, col], sib)
-        wait(s.at[g, 0], recv_g.at[g, col, 1])
-        half(g, above, 5, recv_g.at[g, col, 2], gm)
-        whole(g, above, recv_b.at[g, col], sib)
-
-    def last_g(g, col):
-        wait(s.at[g, 0], recv_g.at[g, col, 2])
-        whole(g, blk(offs[col], 2), recv_b.at[g, col], sib)
+        wait(s.at[g, 0, 0, 0], recv_f.at[g, 2])
+
+    def col(n):
+        return (f + (0, 3, 1, 2)[n]) % 4
+
+    def start_g(g, n):
+        ship_s(g, (col(n), gg), recv_g.at[g, n, 0], gp)
+        ship_s(g, (col(n), gg), recv_g.at[g, n, 1], gm)
+
+    def pass_g(g, n):
+        wait(s.at[g, 0, 0, 0], recv_g.at[g, n, 0])
+        ship_s(g, (col(n), (gg + 3) % 4, pl.ds(0, 5)), recv_g.at[g, n, 2], gp)
+        wait(s.at[g, 0, 0, 0], recv_g.at[g, n, 1])
+        ship_s(g, (col(n), (gg + 1) % 4, pl.ds(5, 5)), recv_g.at[g, n, 2], gm)
+
+    def last_g(g, n):
+        wait(s.at[g, 0, 0, 0], recv_g.at[g, n, 2])
+        ship_s(g, (col(n),), recv_b.at[g, n], sib)
+
+    def from_sibling(g):
+        for n in range(4):
+            wait(s.at[g, 0, 0], recv_b.at[g, n])
 
     def sort_w():
         for a in range(4):
@@ -128,37 +129,39 @@
             total += jnp.dot(wnat[:, n * 256 : (n + 1) * 256].astype(BF16), perm, preferred_element_type=F32)
         wp[...] = total.astype(BF16)
 
-    def quarter(g, n):
-        if n % 2 == 0:
-            c0 = 16 * (n // 2)
-
-            def widen(b, _):
-                for u in range(ROWS):
-                    tmp[pl.ds(pl.multiple_of((b * ROWS + u) * 16, 16), 16), :] = s[g, b, u, c0 : c0 + 16, :].astype(F32)
-                return 0
-
-            lax.fori_loop(0, 32, widen, 0)
-        for c in range(8):
-            s2[:, c * 128 : (c + 1) * 128] = tmp[pl.ds(8 * (n % 2) + c, 320, stride=16), :].astype(BF16)
-        part = jnp.dot(s2[...], v[n * 1024 : (n + 1) * 1024, :], preferred_element_type=F32)
+    def block(g, b):
+        y1, x1, core = b // 8, b // 2 % 4, b % 2
+        return (g, core) + ((y1, x1) if core else (x1, y1))
+
+    def ladder(g, n):
+        part = [s[block(g, b) + (slice(None), slice(16 * n, 16 * n + 16))] for b in range(32)]
+        turned = jnp.swapaxes(jnp.concatenate(part, axis=0), 0, 1)
+        for c in range(16):
+            s2[:, c * 128 : (c + 1) * 128] = turned[c]
+        got = jnp.dot(s2[...], v[n * 2048 : (n + 1) * 2048, :], preferred_element_type=F32)
         for a in range(4):
             if n == 0:
-                lad[g, a] = part[:, a * 128 : (a + 1) * 128]
+                lad[g, a] = got[:, a * 128 : (a + 1) * 128]
             else:
-                lad[g, a] += part[:, a * 128 : (a + 1) * 128]
-        rows = []
-        for k in range(NK):
-            b0, u0 = divmod(NM * k + 2 * n, ROWS)
-            b1, u1 = divmod(NM * k + 2 * n + 1, ROWS)
-            rows.append(jnp.concatenate([s[g, b0, u0], s[g, b1, u1]], axis=1))
-        got = jnp.dot(wp[...], jnp.concatenate(rows, axis=0), preferred_element_type=F32)
-        cyc[g, n, 0] = got[:, 0:128]
-        cyc[g, n, 1] = got[:, 128:256]
-        for m in range(2):
+                lad[g, a] += got[:, a * 128 : (a + 1) * 128]
+
+    def row_of(g, n):
+        b, u = divmod(n, ROWS)
+        return s[block(g, b) + (u,)]
+
+    def cycle(g):
+        for n in range(4):
+            rows = []
+            for k in range(NK):
+                rows.append(jnp.concatenate([row_of(g, NM * k + 2 * n), row_of(g, NM * k + 2 * n + 1)], axis=1))
+            got = jnp.dot(wp[...], jnp.concatenate(rows, axis=0), preferred_element_type=F32)
+            cyc[g, n, 0] = got[:, 0:128]
+            cyc[g, n, 1] = got[:, 128:256]
+
+    def direct(g):
+        for m in range(NM):
             for a in range(4):
-                lad[g, a, pl.ds(2 * n + m, NK, stride=NM), :] += got[
-                    a * NK : (a + 1) * NK, m * 128 : (m + 1) * 128
-                ]
+                lad[g, a, pl.ds(m, NK, stride=NM), :] += cyc[g, m // 2, m % 2, a * NK : (a + 1) * NK, :]
 
     def rows_of(t):
         return pl.ds(pl.multiple_of(t * 80, 80), 80)
@@ -177,17 +180,21 @@
         wait(red_in.at[g, n], recv_r.at[g, n])
         return decode(red_in.at[g, n])
 
-    def reduce_1(g):
-        ship(g, 0, lad_of(g, far), up)
+    def cyc_1(g):
         ship(g, 2, cyc_of(g, far), down)
         ship(g, 1, cyc_of(g, up), up)
+
+    def cyc_2(g):
+        ship(g, 5, cyc_of(g, down) + take(g, 2), down)
+
+    def lad_1(g):
+        ship(g, 0, lad_of(g, far), up)
         ship(g, 3, lad_of(g, down), down)
 
-    def reduce_2(g):
+    def lad_2(g):
         ship(g, 4, lad_of(g, up) + take(g, 0), up)
-        ship(g, 5, cyc_of(g, down) + take(g, 2), down)
-
-    def reduce_3(g):
+
+    def cyc_3(g):
         whole_cyc = (cyc_of(g, r) + take(g, 1) + take(g, 5)).reshape(2, 160, 128)
         for b in range(4):
             val = whole_cyc[:, b * NK : (b + 1) * NK, :].reshape(80, 128)
@@ -197,12 +204,14 @@
             msg[pl.ds(b, 128, stride=4), :] = jnp.concatenate([code, jnp.broadcast_to(log, (48, 128))], axis=0).T
         msg_out[g] = msg[...].astype(jnp.int32).astype(jnp.int16).reshape(32, 16, 128)
         msg_in[g, p] = msg_out[g, p]
+
+    def lad_3(g):
         total = (lad_of(g, r) + take(g, 3) + take(g, 4)).reshape(4, 80, 128)
         for i in range(10):
             for a in range(4):
                 fin[a, pl.ds(i * NK + g, NM, stride=NG), :] = total[a, i * NM : (i + 1) * NM, :]
 
-    batches = ((0, NG - 1), (NG - 1, 1))
+    batches = ((0, NG - 2), (NG - 2, 2))
 
     def exchange(n):
         at = pl.ds(*batches[n])
@@ -228,82 +237,124 @@
                 mir[a, pl.ds(pl.multiple_of((NG * m + g) * NK, 8), NK), :] = val[m * NK : (m + 1) * NK]
 
     start_f(0)
+    start_g(0, 0)
+    for g in range(1, NG):
+        own(g)
+    start_f(1)
+    pass_f(0)
+    start_g(0, 1)
+    start_g(0, 2)
+    last_f(0)
+    start_g(0, 3)
 
     def step(it, _):
-        new, old, done = it, it - 1, it - 2
-        is_new, is_old, is_done = it < NG, (it >= 1) & (it <= NG), it >= 2
-
-        @pl.when(is_new)
-        def _():
-            start_g(new, 0)
-
-        @pl.when(is_old)
-        def _():
-            pass_g(old, 2)
-            last_g(old, 0)
-
-        @pl.when(is_done)
-        def _():
-            for col in range(4):
-                wait(s.at[done, pl.ds(0, 4)], recv_b.at[done, col])
-            quarter(done, 0)
-
-        @pl.when(is_new)
-        def _():
-            pass_f(new)
-            start_g(new, 1)
-
-        @pl.when(it == 1)
+        done, ahead, back = it - 2, it + 1 < NG, it >= 1
+
+        pl.when(it + 2 < NG)(lambda: start_f(it + 2))
+        pl.when(ahead)(lambda: start_g(it + 1, 0))
+        pass_g(it, 0)
+        pl.when(it >= 2)(lambda: last_g(done, 3))
+
+        @pl.when(ahead)
+        def _():
+            pass_f(it + 1)
+            start_g(it + 1, 1)
+
+        pass_g(it, 1)
+        pl.when(back)(lambda: last_g(it - 1, 0))
+
+        @pl.when(it >= 2)
+        def _():
+            from_sibling(done)
+            cycle(done)
+            cyc_1(done)
+
+        pl.when(ahead)(lambda: start_g(it + 1, 2))
+        pass_g(it, 2)
+        pl.when(back)(lambda: last_g(it - 1, 1))
+
+        @pl.when(it == 0)
         def _():
             sort_w()
             wait(v, v_sem)
 
-        @pl.when(is_old)
-        def _():
-            pass_g(old, 3)
-            last_g(old, 1)
-
-        pl.when(is_done)(lambda: quarter(done, 1))
-        pl.when(it >= 3)(lambda: reduce_2(it - 3))
-
-        @pl.when(is_new)
-        def _():
-            pass_g(new, 0)
-            start_g(new, 2)
-
-        pl.when(is_old)(lambda: last_g(old, 2))
-        pl.when(is_done)(lambda: quarter(done, 2))
-        pl.when(it + 1 < NG)(lambda: start_f(it + 1))
-
-        @pl.when(is_new)
-        def _():
-            last_f(new)
-            start_g(new, 3)
-            pass_g(new, 1)
-
-        pl.when(is_old)(lambda: last_g(old, 3))
-
-        @pl.when(is_done)
-        def _():
-            quarter(done, 3)
-            reduce_1(done)
-
-        pl.when(it >= 3)(lambda: reduce_3(it - 3))
+        @pl.when(it >= 2)
+        def _():
+            ladder(done, 0)
+
+        @pl.when(it >= 3)
+        def _():
+            cyc_2(it - 3)
+            lad_2(it - 3)
+
+        @pl.when(ahead)
+        def _():
+            last_f(it + 1)
+            start_g(it + 1, 3)
+
+        pass_g(it, 3)
+        pl.when(back)(lambda: last_g(it - 1, 2))
+
+        @pl.when(it >= 2)
+        def _():
+            ladder(done, 1)
+            direct(done)
+            lad_1(done)
+
+        @pl.when(it >= 4)
+        def _():
+            cyc_3(it - 4)
+            lad_3(it - 4)
+
         return 0
 
-    lax.fori_loop(0, NG + 2, step, 0)
+    lax.fori_loop(0, NG, step, 0)
+
+    end = NG - 1
+    last_g(end - 1, 3)
+    last_g(end, 0)
+    from_sibling(end - 1)
+    cycle(end - 1)
+    cyc_1(end - 1)
+    last_g(end, 1)
+    ladder(end - 1, 0)
+    last_g(end, 2)
+    last_g(end, 3)
+    cyc_2(end - 2)
+    lad_2(end - 2)
+    ladder(end - 1, 1)
+    direct(end - 1)
+    cyc_3(end - 3)
+    lad_3(end - 3)
+    from_sibling(end)
+    cycle(end)
+    cyc_1(end)
+    lad_1(end - 1)
+    cyc_2(end - 1)
+    ladder(end, 0)
+    cyc_3(end - 2)
     exchange(0)
-    reduce_2(NG - 1)
-    reduce_3(NG - 1)
-    exchange(1)
+    ladder(end, 1)
+    direct(end)
+    lad_1(end)
+    cyc_2(end)
+    lad_2(end - 1)
+    lad_3(end - 2)
+    cyc_3(end - 1)
     exchanged(0)
 
-    @pl.loop(0, NG - 1)
+    @pl.loop(0, NG - 2)
     def _(g):
         mirror(g)
 
+    lad_2(end)
+    cyc_3(end)
+    exchange(1)
+    lad_3(end - 1)
+    lad_3(end)
     exchanged(1)
-    mirror(NG - 1)
+    mirror(end - 1)
+    mirror(end)
 
     @pl.loop(0, 10)
     def _(i):
@@ -315,7 +366,9 @@
             out_ref[i, :, lanes] = (residual / denom).astype(BF16)
 
     for g in range(NG):
-        wait(s.at[g, pl.ds(0, 31)], send_s.at[g])
+        wait(s.at[g, 0], send_s.at[g])
+        wait(s.at[g, 0, pl.ds(0, 3)], send_s.at[g])
+        wait(s.at[g, 0, 0, pl.ds(0, 3)], send_s.at[g])
         wait(red_out.at[g], send_r.at[g])
     for n in range(2):
         wait(msg_out.at[pl.ds(*batches[n]), pl.ds(0, 31)], send_m.at[n])
@@ -331,12 +384,12 @@
         in_specs=[vmem, vmem, pl.BlockSpec(memory_space=pl.ANY), vmem, vmem, vmem, vmem, smem, smem],
         out_specs=vmem,
         scratch_shapes=[
-            pltpu.VMEM((NG, 32, ROWS, NC, 128), BF16),
+            pltpu.VMEM((NG, 2, 4, 4, ROWS, NC, 128), BF16),
             pltpu.VMEM((4096, 512), BF16),
             pltpu.VMEM((160, 1280), F32),
             pltpu.VMEM((160, 1280), BF16),
-            pltpu.VMEM((320 * 16, 128), F32),
-            pltpu.VMEM((320, 1024), BF16),
+            pltpu.VMEM((50 * NC, 128), F32),
+            pltpu.VMEM((320, 2048), BF16),
             pltpu.VMEM((NG, 4, 320, 128), F32),
             pltpu.VMEM((NG, 4, 2, 160, 128), F32),
             pltpu.VMEM((NG, 6, 336, 128), jnp.int16),

time: 87.6 us -> 79.3 us (0.905)
  Pallas kernels: 82.2 us -> 73.9 us
    pallas_call x1, Pallas kernels: 82.2 us -> 73.9 us  [fused(): pl.pallas_call(kernel, out_shape=jax.ShapeDtypeStruct((10, NK, 512), BF16...]
where the time goes in v3:
time: 79.3 us; the launch traced here: 79.1 us
  Pallas kernels  73.9 us (93%)
  local copies, waits for them, and re-layouts  5.05 us (6%)
    pallas_call x1, Pallas kernels, fused(): pl.pallas_call(kernel, out_shape=jax.ShapeDtypeStruct((10, NK, 512), BF16...  73.9 us
    unnamed x2, local copies, waits for them, and re-layouts  2.67 us

profile of v3, /device:TPU:1, one launch (start us, length us, event | category | flops | bytes accessed | tf_op | source)
XLA Modules:
  0.0 79.1 jit_solution(17755868827102112721)
XLA Ops:
  0.0 1.3 %copy.12.occ_ref = f32[40,1]{1,0:T(8,128)} copy(f32[40,1]{0,1:T(1,128)} %bitcast.9) | data formatting | bytes 320 | tf_op jit(solution)/shard_map/reshape | solution.py:416
  1.3 0.9 %copy.10 = s32[40,40,2,2]{1,0,3,2:T(8,128)S(1)} copy(s32[40,40,2,2]{1,3,2,0:T(2,128)} %param.8) | data formatting | bytes 51200 | tf_op args[1]
  2.2 0.1 reshape.14
  2.3 0.1 convert_bitcast_fusion
  2.4 0.1 copy.11
  2.5 0.1 broadcast_in_dim.3
  2.7 0.7 reshape.15.mask_ref
  3.4 73.9 %shard_map.73 = bf16[10,40,512]{2,1,0:T(8,128)(2,1)} custom-call(bf16[50,4096]{1,0:T(8,128)(2,1)} %amp_ref.1, f32[50,128]{1,0:T(8,128)} %reshape.15.mask_ref, bf16[4096,512]{1,0:T(8,128)(2,1)} %v_hbm.1, bf16[4,40,1280]{2,1,0:T(8,128)(2,1)} %w_ref.1, bf16[10,40,512]{2,1,0:T(8,128)(2,1)} %coul_ref.1, f32[40,1]{1,0:T(8,128)} %copy.12.occ_ref, ...), custom_call_target="tpu_custom_call" | custom-call | tf_op jit(solution)/shard_map/pallas_call | solution.py:381
  77.3 1.8 %copy.14 = bf16[10,40,512]{2,1,0:T(8,128)(2,1)} copy(bf16[10,40,512]{2,1,0:T(8,128)(2,1)} %shard_map.73) | data formatting | bytes 819200

commit v4 on v3

v4 whole, which is shorter than its diff:
```python
import jax
import jax.numpy as jnp
from jax import lax
from jax.experimental import pallas as pl
from jax.experimental.pallas import tpu as pltpu
from jax.sharding import PartitionSpec as P

NU = 10
NG = 6
NM = 4
NK = 40
STEPS = 32512.0
ROWS = 5
NC = 32
F32 = jnp.float32
BF16 = jnp.bfloat16
MESH = pl.DeviceIdType.MESH


def units(g):
    return (g + 4, 1) if isinstance(g, int) and g >= 4 else (2 * g, 2)


def encode(dst, val):
    rows = val.shape[0]
    size = jnp.maximum(jnp.max(jnp.abs(val), axis=0, keepdims=True), 1e-30)
    log = jnp.ceil(jnp.log(size) * 128.0)
    dst[0:rows] = jnp.round(val * (jnp.exp(log * (-1 / 128)) * STEPS)).astype(jnp.int32).astype(jnp.int16)
    dst[rows : rows + 16] = jnp.broadcast_to(log, (16, 128)).astype(jnp.int32).astype(jnp.int16)


def decode(src):
    rows = src.shape[0] - 16
    log = src[rows : rows + 16].astype(jnp.int32).astype(F32)[0:1]
    return src[0:rows].astype(jnp.int32).astype(F32) * (jnp.exp(log * (1 / 128)) * (1 / STEPS))


def kernel(
    amp_ref, mask_ref, v_hbm, w_ref, coul_ref, vir_ref, occ_smem, vir_smem, out_ref,
    s, v, mask, occ, wnat, wp, tmp, s2, lad, cyc, red_out, red_in, total, msg, z, msg_out, msg_in, fin, mir,
    v_sem, send_s, recv_f, recv_g, recv_b, send_r, recv_r, send_m, recv_m,
):
    p = lax.axis_index("pair")
    r = lax.axis_index("rep")
    h = p % 2
    x = (p // 2) % 4
    y = p // 8
    f = x + h * (y - x)
    gg = y + h * (x - y)
    sf = 1 + 3 * h
    sg = 4 - 3 * h

    def dev(df, dg):
        return 2 * (((f + df) % 4) * sf + ((gg + dg) % 4) * sg) + h

    sib = p + 1 - 2 * h
    fp, fm, gp, gm = dev(1, 0), dev(3, 0), dev(0, 1), dev(0, 3)
    up, down, far = (r + 1) % 4, (r + 3) % 4, (r + 2) % 4

    pltpu.make_async_copy(v_hbm, v, v_sem).start()

    barrier = pltpu.get_barrier_semaphore()

    @pl.loop(1, 32)
    def _(n):
        pl.semaphore_signal(barrier, inc=1, device_id=((p + n) % 32, r), device_id_type=MESH)

    for q in (up, down):
        pl.semaphore_signal(barrier, inc=1, device_id=(p, q), device_id_type=MESH)

    k0 = 5 * p // 4
    tile = (lax.broadcasted_iota(jnp.int32, (2, 128), 1) >= 64).astype(jnp.int32)
    spread = (lax.broadcasted_iota(jnp.int32, (2, 128), 0) == tile).astype(F32)
    for k in range(2):
        mask[k * NK : (k + 1) * NK, :] = lax.dot_general(
            mask_ref[k0 + k, r // 2].astype(F32), spread, (((0,), (0,)), ((), ())), preferred_element_type=F32
        )
    own_mask = mask[pl.ds(50 * p - 40 * k0, 50), :]

    for c in range(NC):
        piece = amp_ref[:, c * 128 : (c + 1) * 128].astype(F32) * own_mask
        tmp[pl.ds(c, 50, stride=NC), :] = piece

    def own(e):
        for u in range(ROWS):
            n = u * NU + e
            s[e, h, f, gg, u] = tmp[n * NC : (n + 1) * NC, :].astype(BF16)

    own(0)
    own(1)
    pl.semaphore_wait(barrier, 33)

    def send(src, dst, ssem, rsem, dev):
        pltpu.make_async_remote_copy(
            src_ref=src, dst_ref=dst, send_sem=ssem, recv_sem=rsem, device_id=dev, device_id_type=MESH
        ).start()

    def wait(ref, sem):
        pltpu.make_async_copy(ref, ref, sem).wait()

    def whole(g, at, sem, to):
        e, n = units(g)
        part = s.at[(pl.ds(e, n), h) + at]
        send(part, part, send_s.at[g], sem, (to, r))

    def half(g, n, at, sem, to):
        e, double = units(g)
        if double == 2:
            part = s.at[(e + n, h) + at]
        else:
            part = s.at[(e, h) + at + (pl.ds(3 * n, 3 - n),)]
        send(part, part, send_s.at[g], sem, (to, r))

    def wait_s(g, at, sem):
        wait(s.at[(pl.ds(0, units(g)[1]), 0) + at], sem)

    def start_f(g):
        whole(g, (f, gg), recv_f.at[g, 0], fp)
        whole(g, (f, gg), recv_f.at[g, 1], fm)

    def pass_f(g):
        wait_s(g, (0, 0), recv_f.at[g, 0])
        half(g, 0, ((f + 3) % 4, gg), recv_f.at[g, 2], fp)
        wait_s(g, (0, 0), recv_f.at[g, 1])
        half(g, 1, ((f + 1) % 4, gg), recv_f.at[g, 2], fm)

    def last_f(g):
        wait_s(g, (0, 0), recv_f.at[g, 2])

    def col(n):
        return (f + (0, 3, 1, 2)[n]) % 4

    def start_g(g, n):
        whole(g, (col(n), gg), recv_g.at[g, n, 0], gp)
        whole(g, (col(n), gg), recv_g.at[g, n, 1], gm)

    def pass_g(g, n):
        wait_s(g, (0, 0), recv_g.at[g, n, 0])
        half(g, 0, (col(n), (gg + 3) % 4), recv_g.at[g, n, 2], gp)
        wait_s(g, (0, 0), recv_g.at[g, n, 1])
        half(g, 1, (col(n), (gg + 1) % 4), recv_g.at[g, n, 2], gm)

    def last_g(g, n):
        wait_s(g, (0, 0), recv_g.at[g, n, 2])
        whole(g, (col(n),), recv_b.at[g, n], sib)

    def from_sibling(g):
        for n in range(4):
            wait_s(g, (0,), recv_b.at[g, n])

    def sort_w():
        for a in range(4):
            wnat[a * NK : (a + 1) * NK, :] = w_ref[a].astype(F32)
        total = jnp.zeros((160, 1280), F32)
        for n in range(5):
            row = n * 256 + lax.broadcasted_iota(jnp.int32, (256, 1280), 0)
            col = lax.broadcasted_iota(jnp.int32, (256, 1280), 1)
            perm = (row == (col & 31) * NK + (col >> 5)).astype(F32).astype(BF16)
            total += jnp.dot(wnat[:, n * 256 : (n + 1) * 256].astype(BF16), perm, preferred_element_type=F32)
        wp[...] = total.astype(BF16)

    def block(e, b):
        y1, x1, core = b // 8, b // 2 % 4, b % 2
        return (e, core) + ((y1, x1) if core else (x1, y1))

    def ladder(g, n):
        e0, double = units(g)
        part = [
            s[block(e0 + e, b) + (slice(None), slice(16 * n, 16 * n + 16))] for e in range(double) for b in range(32)
        ]
        turned = jnp.swapaxes(jnp.concatenate(part, axis=0), 0, 1)
        rows = 160 * double
        for c in range(16):
            s2[0:rows, c * 128 : (c + 1) * 128] = turned[c]
        got = jnp.dot(s2[0:rows, :], v[n * 2048 : (n + 1) * 2048, :], preferred_element_type=F32)
        for e in range(double):
            for a in range(4):
                val = got[e * 160 : (e + 1) * 160, a * 128 : (a + 1) * 128]
                if n == 0:
                    lad[e0 + e, a] = val
                else:
                    lad[e0 + e, a] += val

    def row_of(e, n):
        b, u = divmod(n, ROWS)
        return s[block(e, b) + (u,)]

    def cycle(g):
        e0, double = units(g)
        for e in range(double):
            for m in (0, 2):
                rows = [
                    jnp.concatenate([row_of(e0 + e, NM * k + m), row_of(e0 + e, NM * k + m + 1)], axis=1)
                    for k in range(NK)
                ]
                got = jnp.dot(wp[...], jnp.concatenate(rows, axis=0), preferred_element_type=F32)
                cyc[e0 + e, m] = got[:, 0:128]
                cyc[e0 + e, m + 1] = got[:, 128:256]

    def direct(g):
        e0, double = units(g)
        for e in range(double):
            for m in range(NM):
                for a in range(4):
                    lad[e0 + e, a, pl.ds(m, NK, stride=NM), :] += cyc[e0 + e, m, a * NK : (a + 1) * NK, :]

    def lad_of(g, t):
        e, n = units(g)
        return lad[pl.ds(e, n), :, pl.ds(pl.multiple_of(t * NK, 8), NK), :].reshape(160 * n, 128)

    def cyc_of(g, t):
        e, n = units(g)
        return cyc[pl.ds(e, n), t].reshape(160 * n, 128)

    def coded(buf, g, n):
        return buf.at[g, n, pl.ds(0, 160 * units(g)[1] + 16)]

    def ship(g, n, val, to):
        encode(coded(red_out, g, n), val)
        send(coded(red_out, g, n), coded(red_in, g, n), send_r.at[g], recv_r.at[g, n], (p, to))

    def take(g, n):
        wait(coded(red_in, g, n), recv_r.at[g, n])
        return decode(coded(red_in, g, n))

    def cyc_far(g):
        ship(g, 2, cyc_of(g, far), down)

    def cyc_near(g):
        ship(g, 1, cyc_of(g, up), up)

    def cyc_1(g):
        cyc_far(g)
        cyc_near(g)

    def cyc_2(g):
        ship(g, 5, cyc_of(g, down) + take(g, 2), down)

    def lad_far(g):
        ship(g, 0, lad_of(g, far), up)

    def lad_near(g):
        ship(g, 3, lad_of(g, down), down)

    def lad_1(g):
        lad_far(g)
        lad_near(g)

    def lad_2(g):
        ship(g, 4, lad_of(g, up) + take(g, 0), up)

    def cyc_3(g):
        n = units(g)[1]
        whole_cyc = (cyc_of(g, r) + take(g, 1) + take(g, 5)).reshape(n, 160, 128)
        for b in range(4):
            val = whole_cyc[:, b * NK : (b + 1) * NK, :].reshape(n * NK, 128)
            size = jnp.maximum(jnp.max(jnp.abs(val), axis=0, keepdims=True), 1e-30)
            log = jnp.ceil(jnp.log(size) * 128.0)
            code = jnp.round(val * (jnp.exp(log * (-1 / 128)) * STEPS))
            msg[pl.ds(b, 128, stride=4), :] = jnp.concatenate(
                [code, jnp.broadcast_to(log, (128 - n * NK, 128))], axis=0
            ).T
        msg_out[g] = msg[...].astype(jnp.int32).astype(jnp.int16).reshape(32, 16, 128)
        msg_in[g, p] = msg_out[g, p]

    def lad_3(g):
        e0, n = units(g)
        total[0 : 160 * n, :] = lad_of(g, r) + take(g, 3) + take(g, 4)
        for e in range(n):
            for a in range(4):
                for i in range(10):
                    at = (e * 4 + a) * NK + i * NM
                    fin[a, pl.ds(i * NK + e0 + e, NM, stride=NU), :] = total[at : at + NM, :]

    batches = ((0, 2), (2, 3), (5, 1))

    def exchange(n):
        at = pl.ds(*batches[n])

        @pl.loop(1, 32)
        def _(d):
            to = (p + d) % 32
            send(msg_out.at[at, to], msg_in.at[at, p], send_m.at[n], recv_m.at[n], (to, r))

    def exchanged(n):
        part = msg_in.at[pl.ds(*batches[n]), pl.ds(0, 31)]
        wait(part, recv_m.at[n])

    def mirror(g):
        e0, n = units(g)
        msg[...] = msg_in[g].reshape(512, 128).astype(jnp.int32).astype(F32)
        for a in range(4):
            for b in range(4):
                z[a, pl.ds(b, 32, stride=4), :] = msg[pl.ds(a * 4 + b, 32, stride=16), :]
        for a in range(4):
            turned = z[a].T
            rows = n * NK
            val = turned[0:rows] * (jnp.exp(turned[rows : rows + 1] * (1 / 128)) * (1 / STEPS))
            for e in range(n):
                mir[a, pl.ds(pl.multiple_of((e0 + e) * NK, 8), NK), :] = val[e * NK : (e + 1) * NK]

    start_f(0)
    start_g(0, 0)
    for e in range(2, NU):
        own(e)
    start_f(1)
    pass_f(0)
    start_g(0, 1)
    start_g(0, 2)
    last_f(0)
    start_g(0, 3)

    def step(it, _):
        done, ahead, back, small = it - 2, it < 3, it >= 1, it == 3

        pl.when(it < 2)(lambda: start_f(it + 2))
        pl.when(it == 2)(lambda: start_f(4))
        pl.when(small)(lambda: start_f(5))
        pl.when(ahead)(lambda: start_g(it + 1, 0))
        pl.when(small)(lambda: start_g(4, 0))
        pass_g(it, 0)
        pl.when(it >= 2)(lambda: last_g(done, 3))

        @pl.when(ahead)
        def _():
            pass_f(it + 1)
            start_g(it + 1, 1)

        @pl.when(small)
        def _():
            pass_f(4)
            start_g(4, 1)

        pass_g(it, 1)
        pl.when(back)(lambda: last_g(it - 1, 0))

        @pl.when(it >= 2)
        def _():
            from_sibling(done)
            cycle(done)
            cyc_1(done)

        pl.when(ahead)(lambda: start_g(it + 1, 2))
        pl.when(small)(lambda: start_g(4, 2))
        pass_g(it, 2)
        pl.when(back)(lambda: last_g(it - 1, 1))

        @pl.when(it == 0)
        def _():
            sort_w()
            for j in range(NK):
                occ[j : j + 1, :] = jnp.full((1, 128), occ_smem[j], F32)
            wait(v, v_sem)

        pl.when(it >= 2)(lambda: ladder(done, 0))

        @pl.when(it >= 3)
        def _():
            cyc_2(it - 3)
            lad_2(it - 3)

        @pl.when(ahead)
        def _():
            last_f(it + 1)
            start_g(it + 1, 3)

        @pl.when(small)
        def _():
            last_f(4)
            start_g(4, 3)

        pass_g(it, 3)
        pl.when(back)(lambda: last_g(it - 1, 2))

        @pl.when(it >= 2)
        def _():
            ladder(done, 1)
            direct(done)
            lad_1(done)

        return 0

    lax.fori_loop(0, 4, step, 0)

    start_g(5, 0)
    pass_g(4, 0)
    last_g(2, 3)
    pass_f(5)
    start_g(5, 1)
    pass_g(4, 1)
    last_g(3, 0)
    from_sibling(2)
    cycle(2)
    cyc_1(2)
    start_g(5, 2)
    pass_g(4, 2)
    last_g(3, 1)
    last_f(5)
    start_g(5, 3)
    pass_g(4, 3)
    last_g(3, 2)
    ladder(2, 0)
    pass_g(5, 0)
    last_g(3, 3)
    cyc_2(1)
    lad_2(1)
    ladder(2, 1)
    direct(2)
    lad_1(2)
    pass_g(5, 1)
    last_g(4, 0)
    cyc_3(0)
    lad_3(0)
    from_sibling(3)
    cycle(3)
    cyc_1(3)
    pass_g(5, 2)
    last_g(4, 1)
    pass_g(5, 3)
    last_g(4, 2)
    ladder(3, 0)
    last_g(4, 3)
    last_g(5, 0)
    cyc_2(2)
    ladder(3, 1)
    direct(3)
    lad_1(3)
    last_g(5, 1)
    last_g(5, 2)
    last_g(5, 3)
    lad_2(2)
    from_sibling(4)
    cycle(4)
    cyc_far(4)
    from_sibling(5)
    cycle(5)
    cyc_far(5)
    cyc_2(3)
    cyc_near(4)
    cyc_3(1)
    exchange(0)
    ladder(4, 0)
    ladder(4, 1)
    direct(4)
    lad_1(4)
    lad_2(3)
    cyc_2(4)
    cyc_2(5)
    ladder(5, 0)
    ladder(5, 1)
    direct(5)
    lad_far(5)
    cyc_near(5)
    lad_near(5)
    cyc_3(2)
    lad_3(1)
    lad_2(4)
    cyc_3(3)
    cyc_3(4)
    exchange(1)
    lad_2(5)
    cyc_3(5)
    exchange(2)
    lad_3(2)
    lad_3(3)
    exchanged(0)
    mirror(0)
    mirror(1)
    lad_3(4)
    exchanged(1)
    for g in (2, 3, 4):
        mirror(g)
    lad_3(5)
    exchanged(2)
    mirror(5)

    @pl.loop(0, 10)
    def _(i):
        rows = pl.ds(pl.multiple_of(i * NK, 8), NK)
        for a in range(4):
            lanes = slice(a * 128, (a + 1) * 128)
            residual = coul_ref[i, :, lanes].astype(F32) + fin[a, rows, :] + mir[a, rows, :]
            denom = (vir_smem[p * 4 + a] + vir_ref[...]) - occ_smem[r * 10 + i] - occ[...]
            out_ref[i, :, lanes] = (residual / denom).astype(BF16)

    for g in range(NG):
        wait_s(g, (), send_s.at[g])
        wait_s(g, (pl.ds(0, 3),), send_s.at[g])
        wait_s(g, (0, pl.ds(0, 3)), send_s.at[g])
        wait(red_out.at[g, :, pl.ds(0, 160 * units(g)[1] + 16)], send_r.at[g])
    for n in range(3):
        wait(msg_out.at[pl.ds(*batches[n]), pl.ds(0, 31)], send_m.at[n])


def fused(amp, mask, v, w, coulomb, eps_occ, eps_vir):
    vmem = pl.BlockSpec(memory_space=pltpu.VMEM)
    smem = pl.BlockSpec(memory_space=pltpu.SMEM)
    dma = pltpu.SemaphoreType.DMA
    return pl.pallas_call(
        kernel,
        out_shape=jax.ShapeDtypeStruct((10, NK, 512), BF16),
        in_specs=[vmem, vmem, pl.BlockSpec(memory_space=pl.ANY), vmem, vmem, vmem, smem, smem],
        out_specs=vmem,
        scratch_shapes=[
            pltpu.VMEM((NU, 2, 4, 4, ROWS, NC, 128), BF16),
            pltpu.VMEM((4096, 512), BF16),
            pltpu.VMEM((80, 128), F32),
            pltpu.VMEM((NK, 128), F32),
            pltpu.VMEM((160, 1280), F32),
            pltpu.VMEM((160, 1280), BF16),
            pltpu.VMEM((50 * NC, 128), F32),
            pltpu.VMEM((320, 2048), BF16),
            pltpu.VMEM((NU, 4, 160, 128), F32),
            pltpu.VMEM((NU, 4, 160, 128), F32),
            pltpu.VMEM((NG, 6, 336, 128), jnp.int16),
            pltpu.VMEM((NG, 6, 336, 128), jnp.int16),
            pltpu.VMEM((320, 128), F32),
            pltpu.VMEM((512, 128), F32),
            pltpu.VMEM((4, 128, 128), F32),
            pltpu.VMEM((NG, 32, 16, 128), jnp.int16),
            pltpu.VMEM((NG, 32, 16, 128), jnp.int16),
            pltpu.VMEM((4, 400, 128), F32),
            pltpu.VMEM((4, 400, 128), F32),
            dma,
            dma((NG,)),
            dma((NG, 3)),
            dma((NG, 4, 3)),
            dma((NG, 4)),
            dma((NG,)),
            dma((NG, 6)),
            dma((3,)),
            dma((3,)),
        ],
        compiler_params=pltpu.CompilerParams(
            collective_id=0, has_side_effects=True, vmem_limit_bytes=60 * 1024 * 1024
        ),
    )(amp, mask, v, w, coulomb, eps_vir.reshape(1, 128), eps_occ, eps_vir)


def shards(amplitude, tile_mask, ladder_ints, cycle_ints, coulomb, eps_occ, eps_vir):
    mask = jnp.transpose(tile_mask, (0, 2, 3, 1))
    return fused(amplitude, mask, ladder_ints, cycle_ints, coulomb, eps_occ, eps_vir)


def solution(mesh):
    placed = (
        P("pair", "rep"),
        P(),
        P("rep", "pair"),
        P("pair", None, "rep"),
        P("rep", None, "pair"),
        P(),
        P(),
    )
    return jax.shard_map(
        shards, mesh=mesh, in_specs=placed, out_specs=P("rep", None, "pair"), check_vma=False
    )
```

time: 79.3 us -> 75.7 us (0.955)
  local copies, waits for them, and re-layouts: 5.05 us -> 1.78 us
    reshape x3 -> x0, local copies, waits for them, and re-layouts: 2.16 us -> none  [the longest x1 1.34 us: fused(): eps_occ.reshape(NK, 1)]
    unnamed x2 -> x1, local copies, waits for them, and re-layouts: 2.67 us -> 1.78 us
where the time goes in v4:
time: 75.7 us; the launch traced here: 75.5 us
  Pallas kernels  73.7 us (97%)
  local copies, waits for them, and re-layouts  1.78 us (2%)
    pallas_call x1, Pallas kernels, fused(): pl.pallas_call(kernel, out_shape=jax.ShapeDtypeStruct((10, NK, 512), BF16...  73.7 us
    unnamed x1, local copies, waits for them, and re-layouts  1.78 us

profile of v4, /device:TPU:1, one launch (start us, length us, event | category | flops | bytes accessed | tf_op | source)
XLA Modules:
  0.0 75.5 jit_solution(3941250133564010653)
XLA Ops:
  0.0 73.7 %shard_map.73 = bf16[10,40,512]{2,1,0:T(8,128)(2,1)} custom-call(bf16[50,4096]{1,0:T(8,128)(2,1)} %amp_ref.1, s32[40,2,2,40]{3,2,1,0:T(2,128)} %bitcast.2, bf16[4096,512]{1,0:T(8,128)(2,1)} %v_hbm.1, bf16[4,40,1280]{2,1,0:T(8,128)(2,1)} %w_ref.1, bf16[10,40,512]{2,1,0:T(8,128)(2,1)} %coul_ref.1, f32[1,128]{1,0:T(1,128)} %bitcast.3, f32[40]{0:T(128)} %occ_smem.1, ...), custom_call_target="tpu_custom_call" | custom-call | tf_op jit(solution)/shard_map/pallas_call | solution.py:499
  73.8 1.8 %copy.9 = bf16[10,40,512]{2,1,0:T(8,128)(2,1)} copy(bf16[10,40,512]{2,1,0:T(8,128)(2,1)} %shard_map.73) | data formatting | bytes 819200

commit v5 on v4

--- a/solution.py
+++ b/solution.py
@@ -36,9 +36,9 @@
 
 
 def kernel(
-    amp_ref, mask_ref, v_hbm, w_ref, coul_ref, vir_ref, occ_smem, vir_smem, out_ref,
-    s, v, mask, occ, wnat, wp, tmp, s2, lad, cyc, red_out, red_in, total, msg, z, msg_out, msg_in, fin, mir,
-    v_sem, send_s, recv_f, recv_g, recv_b, send_r, recv_r, send_m, recv_m,
+    amp_ref, mask_ref, v_hbm, w_hbm, coul_hbm, vir_ref, occ_smem, vir_smem, out_ref,
+    s, v, w_ref, coul_ref, mask, occ, wnat, wp, tmp, s2, lad, cyc, red_out, red_in, total, msg, z, msg_out, msg_in, fin, mir,
+    v_sem, w_sem, coul_sem, send_s, recv_f, recv_g, recv_b, send_r, recv_r, send_m, recv_m,
 ):
     p = lax.axis_index("pair")
     r = lax.axis_index("rep")
@@ -57,7 +57,9 @@
     fp, fm, gp, gm = dev(1, 0), dev(3, 0), dev(0, 1), dev(0, 3)
     up, down, far = (r + 1) % 4, (r + 3) % 4, (r + 2) % 4
 
+    pltpu.make_async_copy(w_hbm, w_ref, w_sem).start()
     pltpu.make_async_copy(v_hbm, v, v_sem).start()
+    pltpu.make_async_copy(coul_hbm, coul_ref, coul_sem).start()
 
     barrier = pltpu.get_barrier_semaphore()
 
@@ -250,8 +252,12 @@
         ship(g, 4, lad_of(g, up) + take(g, 0), up)
 
     def cyc_3(g):
-        n = units(g)[1]
-        whole_cyc = (cyc_of(g, r) + take(g, 1) + take(g, 5)).reshape(n, 160, 128)
+        n = 2
+        if isinstance(g, int) and g == 4:
+            parts = [cyc_of(k, r) + take(k, 1) + take(k, 5) for k in (4, 5)]
+            whole_cyc = jnp.concatenate(parts, axis=0).reshape(n, 160, 128)
+        else:
+            whole_cyc = (cyc_of(g, r) + take(g, 1) + take(g, 5)).reshape(n, 160, 128)
         for b in range(4):
             val = whole_cyc[:, b * NK : (b + 1) * NK, :].reshape(n * NK, 128)
             size = jnp.maximum(jnp.max(jnp.abs(val), axis=0, keepdims=True), 1e-30)
@@ -272,7 +278,7 @@
                     at = (e * 4 + a) * NK + i * NM
                     fin[a, pl.ds(i * NK + e0 + e, NM, stride=NU), :] = total[at : at + NM, :]
 
-    batches = ((0, 2), (2, 3), (5, 1))
+    batches = ((0, 2), (2, 2), (4, 1))
 
     def exchange(n):
         at = pl.ds(*batches[n])
@@ -287,7 +293,7 @@
         wait(part, recv_m.at[n])
 
     def mirror(g):
-        e0, n = units(g)
+        e0, n = 2 * g, 2
         msg[...] = msg_in[g].reshape(512, 128).astype(jnp.int32).astype(F32)
         for a in range(4):
             for b in range(4):
@@ -304,6 +310,7 @@
     for e in range(2, NU):
         own(e)
     start_f(1)
+    start_g(1, 0)
     pass_f(0)
     start_g(0, 1)
     start_g(0, 2)
@@ -313,11 +320,13 @@
     def step(it, _):
         done, ahead, back, small = it - 2, it < 3, it >= 1, it == 3
 
-        pl.when(it < 2)(lambda: start_f(it + 2))
-        pl.when(it == 2)(lambda: start_f(4))
-        pl.when(small)(lambda: start_f(5))
-        pl.when(ahead)(lambda: start_g(it + 1, 0))
-        pl.when(small)(lambda: start_g(4, 0))
+        def start(g):
+            start_f(g)
+            start_g(g, 0)
+
+        pl.when(it < 2)(lambda: start(it + 2))
+        pl.when(it == 2)(lambda: start(4))
+        pl.when(small)(lambda: start(5))
         pass_g(it, 0)
         pl.when(it >= 2)(lambda: last_g(done, 3))
 
@@ -347,10 +356,12 @@
 
         @pl.when(it == 0)
         def _():
+            wait(w_ref, w_sem)
             sort_w()
             for j in range(NK):
                 occ[j : j + 1, :] = jnp.full((1, 128), occ_smem[j], F32)
             wait(v, v_sem)
+            wait(coul_ref, coul_sem)
 
         pl.when(it >= 2)(lambda: ladder(done, 0))
 
@@ -382,7 +393,6 @@
 
     lax.fori_loop(0, 4, step, 0)
 
-    start_g(5, 0)
     pass_g(4, 0)
     last_g(2, 3)
     pass_f(5)
@@ -456,10 +466,9 @@
     lad_3(1)
     lad_2(4)
     cyc_3(3)
-    cyc_3(4)
     exchange(1)
     lad_2(5)
-    cyc_3(5)
+    cyc_3(4)
     exchange(2)
     lad_3(2)
     lad_3(3)
@@ -468,11 +477,11 @@
     mirror(1)
     lad_3(4)
     exchanged(1)
-    for g in (2, 3, 4):
-        mirror(g)
+    mirror(2)
+    mirror(3)
     lad_3(5)
     exchanged(2)
-    mirror(5)
+    mirror(4)
 
     @pl.loop(0, 10)
     def _(i):
@@ -499,11 +508,13 @@
     return pl.pallas_call(
         kernel,
         out_shape=jax.ShapeDtypeStruct((10, NK, 512), BF16),
-        in_specs=[vmem, vmem, pl.BlockSpec(memory_space=pl.ANY), vmem, vmem, vmem, smem, smem],
+        in_specs=[vmem, vmem] + [pl.BlockSpec(memory_space=pl.ANY)] * 3 + [vmem, smem, smem],
         out_specs=vmem,
         scratch_shapes=[
             pltpu.VMEM((NU, 2, 4, 4, ROWS, NC, 128), BF16),
             pltpu.VMEM((4096, 512), BF16),
+            pltpu.VMEM((4, NK, 1280), BF16),
+            pltpu.VMEM((10, NK, 512), BF16),
             pltpu.VMEM((80, 128), F32),
             pltpu.VMEM((NK, 128), F32),
             pltpu.VMEM((160, 1280), F32),
@@ -517,10 +528,12 @@
             pltpu.VMEM((320, 128), F32),
             pltpu.VMEM((512, 128), F32),
             pltpu.VMEM((4, 128, 128), F32),
-            pltpu.VMEM((NG, 32, 16, 128), jnp.int16),
-            pltpu.VMEM((NG, 32, 16, 128), jnp.int16),
+            pltpu.VMEM((5, 32, 16, 128), jnp.int16),
+            pltpu.VMEM((5, 32, 16, 128), jnp.int16),
             pltpu.VMEM((4, 400, 128), F32),
             pltpu.VMEM((4, 400, 128), F32),
+            dma,
+            dma,
             dma,
             dma((NG,)),
             dma((NG, 3)),

time: 75.7 us -> 75.6 us (level)
  no operation moved by 1% of the time
where the time goes in v5:
time: 75.6 us; the launch traced here: 75.5 us
  Pallas kernels  73.7 us (97%)
  local copies, waits for them, and re-layouts  1.78 us (2%)
    pallas_call x1, Pallas kernels, fused(): pl.pallas_call(kernel, out_shape=jax.ShapeDtypeStruct((10, NK, 512), BF16...  73.7 us
    unnamed x1, local copies, waits for them, and re-layouts  1.78 us

profile of v5, /device:TPU:1, one launch (start us, length us, event | category | flops | bytes accessed | tf_op | source)
XLA Modules:
  0.0 75.5 jit_solution(1042904781120778917)
XLA Ops:
  0.0 73.7 %shard_map.73 = bf16[10,40,512]{2,1,0:T(8,128)(2,1)} custom-call(bf16[50,4096]{1,0:T(8,128)(2,1)} %amp_ref.1, s32[40,2,2,40]{3,2,1,0:T(2,128)} %bitcast.2, bf16[4096,512]{1,0:T(8,128)(2,1)} %v_hbm.1, bf16[4,40,1280]{2,1,0:T(8,128)(2,1)} %w_hbm.1, bf16[10,40,512]{2,1,0:T(8,128)(2,1)} %coul_hbm.1, f32[1,128]{1,0:T(1,128)} %bitcast.3, f32[40]{0:T(128)} %occ_smem.1, ...), custom_call_target="tpu_custom_call" | custom-call | tf_op jit(solution)/shard_map/pallas_call | solution.py:508
  73.7 1.8 %copy.9 = bf16[10,40,512]{2,1,0:T(8,128)(2,1)} copy(bf16[10,40,512]{2,1,0:T(8,128)(2,1)} %shard_map.73) | data formatting | bytes 819200
